TPU v7x, 32 devices: a whole 2x2x4 slice. The times are simulated.
32 devices in a mesh: space: 8 (over z, y), chan: 4 (over x, core).
Axes of the slice: x: 2, y: 2, z: 4, core: 2. Of those that a mesh axis runs over, the one named last changes fastest.
Arguments:
- features: bfloat16 [32, 128, 512], P('space', 'chan'), may hold values from -6 to 6
- occupancy: int32 [32, 512], P('space'), may hold values 0 or 1
- weight: bfloat16 [256, 27, 128], P('chan'), may hold values from -0.109375 to 0.109375
- cotangent: bfloat16 [32, 256, 512], P('space', 'chan'), may hold values from -6 to 6
- neighbours: int32 [32, 26], P('space'), may hold values from -1 to 31, as said below
Outputs:
- activation: bfloat16 [32, 256, 512], P('space', 'chan')
- input_grad: bfloat16 [32, 128, 512], P('space', 'chan')
- weight_grad: float32 [256, 27, 128], P('chan')
Inputs may be any that keep to these rules, and one draw needn't show every extreme that they name: `neighbours`: each entry is -1 or a block id. With o = id // 4 the listing block's owner, an entry names a block of owner o, or, only for a listing block among the first 1 of its owner and only in columns 0 to 12, one of the last 1 block of owner o - 1, or, only for a listing block among the last 1 of its owner and only in columns 13 to 25, one of the first 1 block of owner o + 1. The same block may appear in several directions.
All inputs are finite; a program needn't handle non-finite values. No bound on the sum of `occupancy` on one device may be relied on, other than what follows from the above.
Results may differ from a plain program's by a relative error of at most 0.0049.
Values may be sent and summed in bfloat16 or wider, within the bound.
A program may use at most 64 MiB of HBM per device.

v0:
```python
import jax
import jax.numpy as jnp
from jax import lax
from jax.sharding import PartitionSpec as P


def with_halo(block, sides, width):
    for axis, dim in sides:
        count = lax.axis_size(axis)
        forward = [(i, i + 1) for i in range(count - 1)]
        backward = [(target, source) for source, target in forward]
        low = lax.ppermute(
            lax.slice_in_dim(block, block.shape[dim] - width, None, axis=dim), axis, forward
        )
        high = lax.ppermute(lax.slice_in_dim(block, 0, width, axis=dim), axis, backward)
        block = jnp.concatenate([low, block, high], axis=dim)
    return block


def shifted(value, axis, steps):
    count = lax.axis_size(axis)
    first, last = (max(0, -steps), min(count, count - steps))
    return lax.ppermute(value, axis, [(source, source + steps) for source in range(first, last)])


def offset_list():
    return [(a, b, c) for a in (-1, 0, 1) for b in (-1, 0, 1) for c in (-1, 0, 1)]


def build_patches(blocks):
    channels = blocks.shape[1]
    cube_grid = blocks.reshape(3, 3, 3, channels, 8, 8, 8)
    cube_grid = jnp.transpose(cube_grid, (3, 0, 4, 1, 5, 2, 6)).reshape(channels, 24, 24, 24)
    padded = cube_grid[:, 7:17, 7:17, 7:17]
    pieces = [padded[:, 1 + a : 9 + a, 1 + b : 9 + b, 1 + c : 9 + c] for a, b, c in offset_list()]
    return jnp.stack(pieces).reshape(27 * channels, 512)


def fold_back(grad_patches, channels):
    terms = grad_patches.reshape(27, channels, 8, 8, 8)
    padded_grad = jnp.zeros((channels, 10, 10, 10), jnp.float32)
    for offset_id, (a, b, c) in enumerate(offset_list()):
        padded_grad = padded_grad + jnp.pad(
            terms[offset_id], ((0, 0), (1 + a, 1 - a), (1 + b, 1 - b), (1 + c, 1 - c))
        )
    wide_grid = jnp.pad(padded_grad, ((0, 0), (7, 7), (7, 7), (7, 7))).reshape(
        channels, 3, 8, 3, 8, 3, 8
    )
    return jnp.transpose(wide_grid, (1, 3, 5, 0, 2, 4, 6)).reshape(27, channels, 512)


def on_device(features, occupancy, weight, cotangent, neighbours):
    block_count = features.shape[0]
    active_voxel_mask = occupancy.astype(jnp.bfloat16)
    mask_applied = features * active_voxel_mask[:, None, :]
    widened = lax.all_gather(mask_applied, "chan", axis=1, tiled=True)
    enlarged_block = with_halo(widened, (("space", 0),), block_count)
    place = lax.axis_index("space")
    first_local = place * block_count - block_count
    self_ids = (place * block_count + jnp.arange(block_count, dtype=jnp.int32))[:, None]
    every_index_list = jnp.concatenate([neighbours[:, :13], self_ids, neighbours[:, 13:]], axis=1)
    present_all = every_index_list >= 0
    slot_ids = jnp.where(present_all, every_index_list - first_local, 0)
    cout_local = weight.shape[0]
    cin = weight.shape[2]
    weight_flat = weight.reshape(cout_local, 27 * cin)
    contract_last = (((1,), (1,)), ((), ()))
    contract_first = (((0,), (0,)), ((), ()))

    def visit(totals, position):
        weight_running_sum, grad_cubes = totals
        slots = slot_ids[position]
        present = present_all[position]
        blocks = enlarged_block[slots] * present.astype(jnp.bfloat16)[:, None, None]
        patches = build_patches(blocks)
        pre_act = jnp.dot(weight_flat, patches, preferred_element_type=jnp.float32)
        live_row = occupancy[position].astype(jnp.float32)[None, :]
        output = (jax.nn.silu(pre_act) * live_row).astype(jnp.bfloat16)
        sigma = jax.nn.sigmoid(pre_act)
        slope = sigma * (1.0 + pre_act * (1.0 - sigma))
        grad_pre = (cotangent[position].astype(jnp.float32) * slope * live_row).astype(jnp.bfloat16)
        weight_terms = lax.dot_general(
            grad_pre, patches, contract_last, preferred_element_type=jnp.float32
        )
        grad_patches = lax.dot_general(
            weight_flat, grad_pre, contract_first, preferred_element_type=jnp.float32
        )
        pieces = fold_back(grad_patches, cin) * present.astype(jnp.float32)[:, None, None]
        grad_cubes = grad_cubes.at[slots].add(pieces)
        return ((weight_running_sum + weight_terms, grad_cubes), output)

    start = (
        jnp.zeros((cout_local, 27 * cin), jnp.float32),
        jnp.zeros((block_count + 2 * block_count, cin, 512), jnp.float32),
    )
    (weight_running_sum, grad_acc), activation = lax.scan(
        visit, start, jnp.arange(block_count, dtype=jnp.int32)
    )
    rest = block_count - block_count
    sum_reduced = grad_acc[block_count : block_count + block_count]
    for stride, rim_part, spacing in (
        (1, grad_acc[block_count + block_count :], (0, rest)),
        (-1, grad_acc[:block_count], (rest, 0)),
    ):
        arrived = shifted(rim_part.astype(jnp.bfloat16), "space", stride).astype(rim_part.dtype)
        sum_reduced = sum_reduced + arrived
    reduced_own = lax.psum_scatter(sum_reduced, "chan", scatter_dimension=1, tiled=True)
    input_grad = (reduced_own * occupancy.astype(jnp.float32)[:, None, :]).astype(jnp.bfloat16)
    weight_total = lax.psum(weight_running_sum.reshape(cout_local, 27, cin), "space")
    weight_grad = weight_total * lax.rsqrt(jnp.float32(lax.axis_size("space") * block_count * 512))
    return (activation, input_grad, weight_grad)


def solution(mesh):
    placed = (
        P("space", "chan", None),
        P("space", None),
        P("chan", None, None),
        P("space", "chan", None),
        P("space", None),
    )
    return jax.shard_map(
        on_device,
        mesh=mesh,
        in_specs=placed,
        out_specs=(P("space", "chan", None), P("space", "chan", None), P("chan", None, None)),
        check_vma=False,
    )
```

profile of v0, /device:TPU:0, one launch (start us, length us, event | category | flops | bytes accessed | tf_op | source)
XLA Modules:
  0.0 390.5 jit_solution(10731175620392481470)
XLA Ops:
  10.4 8.6 %all_gather.3 = bf16[4,128,512]{2,1,0:T(8,128)(2,1)S(1)} all-gather(bf16[4,32,512]{2,1,0:T(8,128)(2,1)S(1)} %broadcast_multiply_fusion.2), channel_id=1, replica_groups=mesh['space'=8,'chan'=4] {'chan'}, dimensions={1}, use_global_device_ids=true | all-gather | bytes 655360 | tf_op jit(solution)/shard_map/all_gather | solution.py:56
  20.3 5.3 %collective-permute-start = (bf16[4,128,512]{2,1,0:T(8,128)(2,1)S(1)}, bf16[4,128,512]{2,1,0:T(8,128)(2,1)}, u32[]{:S(2)}, u32[]{:S(2)}) collective-permute-start(bf16[4,128,512]{2,1,0:T(8,128)(2,1)S(1)} %all_gather.3), channel_id=1, source_target_pairs={{0,4},{4,8},{8,12},{12,16},{16,20},{20,24},{24,28},{1,5},{5,9},{9,... | collective-permute-start | bytes 1572872 | tf_op jit(solution)/shard_map/ppermute | solution.py:12
  26.7 8.4 %collective-permute-done.1 = bf16[4,128,512]{2,1,0:T(8,128)(2,1)S(1)} collective-permute-done((bf16[4,128,512]{2,1,0:T(8,128)(2,1)S(1)}, bf16[4,128,512]{2,1,0:T(8,128)(2,1)S(1)}, u32[]{:S(2)}, u32[]{:S(2)}) %collective-permute-start.1) | collective-permute-done | bytes 524320 | tf_op jit(solution)/shard_map/ppermute | solution.py:15
  35.8 10.4 %collective-permute-done = bf16[4,128,512]{2,1,0:T(8,128)(2,1)} collective-permute-done((bf16[4,128,512]{2,1,0:T(8,128)(2,1)S(1)}, bf16[4,128,512]{2,1,0:T(8,128)(2,1)}, u32[]{:S(2)}, u32[]{:S(2)}) %collective-permute-start) | collective-permute-done | bytes 524320 | tf_op jit(solution)/shard_map/ppermute | solution.py:12
  49.8 238.1 %while.17 = (s32[]{:T(128)}, f32[64,3456]{1,0:T(8,128)S(1)}, f32[12,128,512]{2,1,0:T(8,128)}, bf16[4,64,512]{2,1,0:T(8,128)(2,1)}, s32[4]{0:T(128)S(1)}, /*index...) while((s32[]{:T(128)}, f32[64,3456]{1,0:T(8,128)S(1)}, ...), condition=%wide.region_2.3_spmd.clone, body=%wide.region_0.2_spmd.clone.sunk | while | flops 689475200 | bytes 152919280 | solution.py:96
  55.8 5.7 %copy.45 = bf16[27,128,512]{1,2,0:T(8,128)(2,1)} copy(bf16[27,128,512]{2,1,0:T(8,128)(2,1)} %gather_fusion) | data formatting | bytes 7077888 | tf_op jit(solution)/shard_map/while/body/eval_jaxpr/gather | solution.py:74
  66.0 4.0 %copy.47 = bf16[27,128,8,8,8]{1,0,4,3,2:T(8,128)(2,1)S(1)} copy(bf16[27,128,8,8,8]{1,4,3,2,0:T(8,128)(2,1)S(1)} %fusion.116) | data formatting | bytes 7077888 | tf_op jit(solution)/shard_map/while/body/eval_jaxpr/stack | solution.py:36
  84.2 8.0 %copy.49 = f32[27,128,512]{2,1,0:T(8,128)} copy(f32[27,128,512]{1,2,0:T(8,128)} %broadcast_multiply_fusion.4) | data formatting | bytes 14155776 | tf_op jit(solution)/shard_map/while/body/eval_jaxpr/mul | solution.py:88
  92.2 17.0 %scatter_fusion = f32[12,128,512]{2,1,0:T(8,128)} fusion(f32[12,128,512]{2,1,0:T(8,128)} %get-tuple-element.386, s32[27]{0:T(128)S(1)} %fusion.89, f32[27,128,512]{2,1,0:T(8,128)} %copy.49), kind=kCustom, calls=%fused_computation.1.clone.clone.1 | custom fusion | flops 1769472 | bytes 21233772 | tf_op jit(solution)/shard_map/while/body/eval_jaxpr/scatter-add | solution.py:89
  115.1 5.7 %copy.45 = bf16[27,128,512]{1,2,0:T(8,128)(2,1)} copy(bf16[27,128,512]{2,1,0:T(8,128)(2,1)} %gather_fusion) | data formatting | bytes 7077888 | tf_op jit(solution)/shard_map/while/body/eval_jaxpr/gather | solution.py:74
  125.4 4.0 %copy.47 = bf16[27,128,8,8,8]{1,0,4,3,2:T(8,128)(2,1)S(1)} copy(bf16[27,128,8,8,8]{1,4,3,2,0:T(8,128)(2,1)S(1)} %fusion.116) | data formatting | bytes 7077888 | tf_op jit(solution)/shard_map/while/body/eval_jaxpr/stack | solution.py:36
  143.6 8.0 %copy.49 = f32[27,128,512]{2,1,0:T(8,128)} copy(f32[27,128,512]{1,2,0:T(8,128)} %broadcast_multiply_fusion.4) | data formatting | bytes 14155776 | tf_op jit(solution)/shard_map/while/body/eval_jaxpr/mul | solution.py:88
  151.5 17.1 %scatter_fusion = f32[12,128,512]{2,1,0:T(8,128)} fusion(f32[12,128,512]{2,1,0:T(8,128)} %get-tuple-element.386, s32[27]{0:T(128)S(1)} %fusion.89, f32[27,128,512]{2,1,0:T(8,128)} %copy.49), kind=kCustom, calls=%fused_computation.1.clone.clone.1 | custom fusion | flops 1769472 | bytes 21233772 | tf_op jit(solution)/shard_map/while/body/eval_jaxpr/scatter-add | solution.py:89
  174.6 5.7 %copy.45 = bf16[27,128,512]{1,2,0:T(8,128)(2,1)} copy(bf16[27,128,512]{2,1,0:T(8,128)(2,1)} %gather_fusion) | data formatting | bytes 7077888 | tf_op jit(solution)/shard_map/while/body/eval_jaxpr/gather | solution.py:74
  184.8 4.0 %copy.47 = bf16[27,128,8,8,8]{1,0,4,3,2:T(8,128)(2,1)S(1)} copy(bf16[27,128,8,8,8]{1,4,3,2,0:T(8,128)(2,1)S(1)} %fusion.116) | data formatting | bytes 7077888 | tf_op jit(solution)/shard_map/while/body/eval_jaxpr/stack | solution.py:36
  203.0 8.0 %copy.49 = f32[27,128,512]{2,1,0:T(8,128)} copy(f32[27,128,512]{1,2,0:T(8,128)} %broadcast_multiply_fusion.4) | data formatting | bytes 14155776 | tf_op jit(solution)/shard_map/while/body/eval_jaxpr/mul | solution.py:88
  211.0 17.2 %scatter_fusion = f32[12,128,512]{2,1,0:T(8,128)} fusion(f32[12,128,512]{2,1,0:T(8,128)} %get-tuple-element.386, s32[27]{0:T(128)S(1)} %fusion.89, f32[27,128,512]{2,1,0:T(8,128)} %copy.49), kind=kCustom, calls=%fused_computation.1.clone.clone.1 | custom fusion | flops 1769472 | bytes 21233772 | tf_op jit(solution)/shard_map/while/body/eval_jaxpr/scatter-add | solution.py:89
  234.2 5.7 %copy.45 = bf16[27,128,512]{1,2,0:T(8,128)(2,1)} copy(bf16[27,128,512]{2,1,0:T(8,128)(2,1)} %gather_fusion) | data formatting | bytes 7077888 | tf_op jit(solution)/shard_map/while/body/eval_jaxpr/gather | solution.py:74
  244.4 4.0 %copy.47 = bf16[27,128,8,8,8]{1,0,4,3,2:T(8,128)(2,1)S(1)} copy(bf16[27,128,8,8,8]{1,4,3,2,0:T(8,128)(2,1)S(1)} %fusion.116) | data formatting | bytes 7077888 | tf_op jit(solution)/shard_map/while/body/eval_jaxpr/stack | solution.py:36
  262.6 8.0 %copy.49 = f32[27,128,512]{2,1,0:T(8,128)} copy(f32[27,128,512]{1,2,0:T(8,128)} %broadcast_multiply_fusion.4) | data formatting | bytes 14155776 | tf_op jit(solution)/shard_map/while/body/eval_jaxpr/mul | solution.py:88
  270.6 17.2 %scatter_fusion = f32[12,128,512]{2,1,0:T(8,128)} fusion(f32[12,128,512]{2,1,0:T(8,128)} %get-tuple-element.386, s32[27]{0:T(128)S(1)} %fusion.89, f32[27,128,512]{2,1,0:T(8,128)} %copy.49), kind=kCustom, calls=%fused_computation.1.clone.clone.1 | custom fusion | flops 1769472 | bytes 21233772 | tf_op jit(solution)/shard_map/while/body/eval_jaxpr/scatter-add | solution.py:89
  291.3 4.8 %collective-permute-start.2 = (bf16[4,128,512]{2,1,0:T(8,128)(2,1)S(1)}, bf16[4,128,512]{2,1,0:T(8,128)(2,1)S(1)}, u32[]{:S(2)}, u32[]{:S(2)}) collective-permute-start(bf16[4,128,512]{2,1,0:T(8,128)(2,1)S(1)} %get-tuple-element.238), channel_id=1, source_target_pairs={{0,4},{4,8},{8,12},{12,16},{16,20},{20,24},{24,28},{1,5},{5,9},{9,... | collective-permute-start | bytes 1572872 | tf_op jit(solution)/shard_map/ppermute | solution.py:23
  297.6 24.1 %collective-permute-done.2 = bf16[4,128,512]{2,1,0:T(8,128)(2,1)S(1)} collective-permute-done((bf16[4,128,512]{2,1,0:T(8,128)(2,1)S(1)}, bf16[4,128,512]{2,1,0:T(8,128)(2,1)S(1)}, u32[]{:S(2)}, u32[]{:S(2)}) %collective-permute-start.2) | collective-permute-done | bytes 524320 | tf_op jit(solution)/shard_map/ppermute | solution.py:23
  324.2 54.5 %all-reduce.30.cloned.1.call-done = f32[64,27,128]{2,1,0:T(8,128)} async-done(((f32[64,27,128]{2,1,0:T(8,128)}), f32[64,27,128]{2,1,0:T(8,128)}) %all-reduce.30.cloned.1.call-update) | async-done | bytes 884752 | tf_op jit(solution)/shard_map/psum | solution.py:109
  (221 shorter events, 110.8 us)
Async XLA Ops:
  8.0 18.6 %copy-start = (bf16[64,27,128]{2,0,1:T(8,128)(2,1)S(1)}, bf16[64,27,128]{2,0,1:T(8,128)(2,1)}, u32[]{:S(2)}) copy-start(bf16[64,27,128]{2,0,1:T(8,128)(2,1)} %param.9) | copy-start | bytes 1327108
  8.0 370.7 %all-reduce.30.cloned.1.call-start = ((), (), s32[]{:S(2)}) async-start(), calls=%async_computation.2 | async-start | bytes 2097152 | tf_op jit(solution)/shard_map/psum | solution.py:109
  19.0 16.1 %copy-start.2 = (bf16[4,128,512]{2,1,0:T(8,128)(2,1)}, bf16[4,128,512]{2,1,0:T(8,128)(2,1)S(1)}, u32[]{:S(2)}) copy-start(bf16[4,128,512]{2,1,0:T(8,128)(2,1)S(1)} %all_gather.3) | copy-start | bytes 1572868
  19.0 16.1 %collective-permute-start.1 = (bf16[4,128,512]{2,1,0:T(8,128)(2,1)S(1)}, bf16[4,128,512]{2,1,0:T(8,128)(2,1)S(1)}, u32[]{:S(2)}, u32[]{:S(2)}) collective-permute-start(bf16[4,128,512]{2,1,0:T(8,128)(2,1)S(1)} %all_gather.3), channel_id=1, source_target_pairs={{4,0},{8,4},{12,8},{16,12},{20,16},{24,20},{28,24},{5,1},{9,5},{13... | collective-permute-start | bytes 1572872 | tf_op jit(solution)/shard_map/ppermute | solution.py:15
  20.3 25.9 %collective-permute-start = (bf16[4,128,512]{2,1,0:T(8,128)(2,1)S(1)}, bf16[4,128,512]{2,1,0:T(8,128)(2,1)}, u32[]{:S(2)}, u32[]{:S(2)}) collective-permute-start(bf16[4,128,512]{2,1,0:T(8,128)(2,1)S(1)} %all_gather.3), channel_id=1, source_target_pairs={{0,4},{4,8},{8,12},{12,16},{16,20},{20,24},{24,28},{1,5},{5,9},{9,... | collective-permute-start | bytes 1572872 | tf_op jit(solution)/shard_map/ppermute | solution.py:12
  35.0 0.8 copy-start.3
  289.1 92.4 %reduce-scatter.2.cloned.1.call-start = ((), (), s32[]{:S(2)}) async-start(), calls=%async_computation.1 | async-start | bytes 1310720 | tf_op jit(solution)/shard_map/reduce_scatter | solution.py:107
  291.3 30.4 %collective-permute-start.2 = (bf16[4,128,512]{2,1,0:T(8,128)(2,1)S(1)}, bf16[4,128,512]{2,1,0:T(8,128)(2,1)S(1)}, u32[]{:S(2)}, u32[]{:S(2)}) collective-permute-start(bf16[4,128,512]{2,1,0:T(8,128)(2,1)S(1)} %get-tuple-element.238), channel_id=1, source_target_pairs={{0,4},{4,8},{8,12},{12,16},{16,20},{20,24},{24,28},{1,5},{5,9},{9,... | collective-permute-start | bytes 1572872 | tf_op jit(solution)/shard_map/ppermute | solution.py:23
  296.1 87.0 %copy-start.1 = (bf16[64,27,128]{2,0,1:T(8,128)(2,1)S(1)}, bf16[64,27,128]{2,0,1:T(8,128)(2,1)}, u32[]{:S(2)}) copy-start(bf16[64,27,128]{2,0,1:T(8,128)(2,1)} %param.9) | copy-start | bytes 1327108
  296.1 85.3 %copy-start.4 = (f32[4,512]{1,0:T(4,128)S(1)}, f32[4,512]{1,0:T(4,128)}, u32[]{:S(2)}) copy-start(f32[4,512]{1,0:T(4,128)} %get-tuple-element.240) | copy-start | bytes 24580
  296.1 25.5 %collective-permute-start.3 = (bf16[4,128,512]{2,1,0:T(8,128)(2,1)S(1)}, bf16[4,128,512]{2,1,0:T(8,128)(2,1)S(1)}, u32[]{:S(2)}, u32[]{:S(2)}) collective-permute-start(bf16[4,128,512]{2,1,0:T(8,128)(2,1)S(1)} %get-tuple-element.239), channel_id=1, source_target_pairs={{4,0},{8,4},{12,8},{16,12},{20,16},{24,20},{28,24},{5,1},{9,5},{13... | collective-permute-start | bytes 1572872 | tf_op jit(solution)/shard_map/ppermute | solution.py:23
Sparse Core Ops, SparseCore 0:
  289.2 89.4 all-reduce.29
Sparse Core Ops, SparseCore 1:
  324.3 26.8 reduce-scatter.1
where the time goes:
time: 392 us; the launch traced here: 391 us
  other arithmetic  111 us (28%)
  local copies, waits for them, and re-layouts  109 us (28%)
  waiting for transfers between devices  97.4 us (25%)
  matrix products  27.7 us (7%)
  between operations  15.6 us (4%)
  starting transfers between devices  12.9 us (3%)
  blocking collectives  8.62 us (2%)
  loops' own time  8.5 us (2%)
    scatter-add x4, other arithmetic, visit(): grad_cubes = grad_cubes.at[slots].add(pieces)  68.5 us
    psum x1, waiting for transfers between devices, on_device(): lax.psum(weight_running_sum.reshape(cout_local, 27, cin), 'space')  54.5 us
    gather x8, local copies, waits for them, and re-layouts, visit(): blocks = enlarged_block[slots] * present.astype(jnp.bfloat16)[:, None, None]  33.3 us
    mul x4, local copies, waits for them, and re-layouts, visit(): fold_back(grad_patches, cin) * present.astype(jnp.float32)[:, None, None]  32 us
    ppermute x2, waiting for transfers between devices, shifted(): lax.ppermute(value, axis, [(source, source + steps) for source in range(f...  24.1 us
    another operation x8, local copies, waits for them, and re-layouts, build_patches(): return jnp.stack(pieces).reshape(27 * channels, 512)  16.4 us
    mul x4, other arithmetic, visit(): fold_back(grad_patches, cin) * present.astype(jnp.float32)[:, None, None]  15 us
    dot_general x4, matrix products, visit(): pre_act = jnp.dot(weight_flat, patches, preferred_element_type=jnp.float32)  10.6 us
  transfers between devices with their start and end apart: 6, of which 4 were waited for; matrix products, arithmetic and copies ran while one was open for 2% of the time, Pallas kernels for 0%

commit v1 on v0

v1 whole, which is shorter than its diff:
```python
import functools

import jax
import jax.numpy as jnp
from jax import lax
from jax.experimental import pallas as pl
from jax.experimental.pallas import tpu as pltpu
from jax.sharding import PartitionSpec as P

MESH = pl.DeviceIdType.MESH
F32 = jnp.float32
BF16 = jnp.bfloat16


def places(space_count):
    s, c = lax.axis_index("space"), lax.axis_index("chan")
    before = lax.rem(s + space_count - 1, space_count)
    after = lax.rem(s + 1, space_count)
    near = c + 1 - 2 * lax.rem(c, 2)
    far = lax.rem(c + 2, 4)
    return s, c, before, after, near, far


def greet(peers):
    barrier = pltpu.get_barrier_semaphore()
    for peer in peers:
        pl.semaphore_signal(barrier, inc=1, device_id=peer, device_id_type=MESH)
    pl.semaphore_wait(barrier, len(peers))


def gather_kernel(space_count, features_ref, occupancy_ref, full_ref, send_sem, recv_sem):
    blocks = features_ref.shape[0]
    s, c, before, after, near, far = places(space_count)

    def copy(slots, piece, to_slots, peer, index):
        return pltpu.make_async_remote_copy(
            src_ref=full_ref.at[slots, piece],
            dst_ref=full_ref.at[to_slots, piece],
            send_sem=send_sem.at[index],
            recv_sem=recv_sem.at[index],
            device_id=peer,
            device_id_type=MESH,
        )

    for b in range(blocks):
        mask = occupancy_ref[b : b + 1].astype(F32)
        full_ref[1 + b, c] = (features_ref[b].astype(F32) * mask).astype(BF16)
    greet([(before, c), (after, c), (s, near), (s, far)])
    own = pl.ds(1, blocks)
    low, high = 0, blocks + 1
    rim_down = copy(1, c, high, (before, c), 0)
    rim_up = copy(blocks, c, low, (after, c), 1)
    own_far = copy(own, c, own, (s, far), 2)
    own_near = copy(own, c, own, (s, near), 3)
    for each in (rim_down, rim_up, own_far, own_near):
        each.start()
    rim_down.wait_recv()
    rim_up.wait_recv()
    high_far = copy(high, c, high, (s, far), 4)
    low_far = copy(low, c, low, (s, far), 5)
    high_near = copy(high, c, high, (s, near), 6)
    low_near = copy(low, c, low, (s, near), 7)
    for each in (high_far, low_far, high_near, low_near):
        each.start()
    own_far.wait_recv()
    own_pass = copy(own, far, own, (s, near), 8)
    own_pass.start()
    high_far.wait_recv()
    low_far.wait_recv()
    high_pass = copy(high, far, high, (s, near), 9)
    low_pass = copy(low, far, low, (s, near), 10)
    high_pass.start()
    low_pass.start()
    for each in (own_near, high_near, low_near, own_pass, high_pass, low_pass):
        each.wait_recv()
    for each in (
        rim_down, rim_up, own_far, own_near, high_far, low_far,
        high_near, low_near, own_pass, high_pass, low_pass,
    ):
        each.wait_send()


def conv_kernel(
    neighbours_ref, full_ref, occupancy_ref, weight_ref, cotangent_ref,
    act_ref, grad_ref, wgrad_ref, cubes, sums, patches, grad_patches, wsum,
):
    blocks = cotangent_ref.shape[0]
    outs = cotangent_ref.shape[1]
    slots = blocks + 2
    place = lax.axis_index("space")
    for slot in range(slots):
        cubes[slot] = full_ref[slot].astype(F32).T.reshape(8, 8, 8, 128)
    cubes[slots] = jnp.zeros((8, 8, 8, 128), F32)
    sums[...] = jnp.zeros(sums.shape, F32)
    wsum[...] = jnp.zeros(wsum.shape, F32)
    k = lax.broadcasted_iota(jnp.int32, (10, 8, 128), 1)
    blank = jnp.zeros((1, 8, 128), F32)

    def visit(p, carry):
        slot = {}
        for number in range(27):
            a, b, c = number // 9 - 1, number // 3 % 3 - 1, number % 3 - 1
            if number == 13:
                slot[a, b, c] = p + 1
            else:
                named = neighbours_ref[p, number - (number > 13)]
                slot[a, b, c] = jnp.where(named < 0, slots, named - place * blocks + 1)

        def plane_of(row):
            a = -1 if row == 0 else (1 if row == 9 else 0)
            return a, (row - 1) % 8

        for row in range(10):
            a, i = plane_of(row)

            def line(c):
                return jnp.concatenate(
                    [cubes[slot[a, -1, c], i, 7:8], cubes[slot[a, 0, c], i], cubes[slot[a, 1, c], i, 0:1]],
                    axis=0,
                )

            middle = line(0)
            views = (
                pltpu.roll(jnp.where(k == 7, line(-1), middle), 1, 1),
                middle,
                pltpu.roll(jnp.where(k == 0, line(1), middle), 7, 1),
            )
            for b in range(3):
                for c in range(3):
                    piece = views[c][b : b + 8].reshape(64, 128).astype(BF16)
                    patches[64 * row : 64 * row + 64, (3 * b + c) * 128 : (3 * b + c + 1) * 128] = piece

        weight = weight_ref[...]
        product = lax.dot_general(
            weight, patches[...], (((1,), (1,)), ((), ())), preferred_element_type=F32
        )
        pre_act = (
            product[:outs, 0:512] + product[outs : 2 * outs, 64:576] + product[2 * outs :, 128:640]
        )
        live = occupancy_ref[p].astype(F32)
        sigma = jax.nn.sigmoid(pre_act)
        act_ref[p] = (pre_act * sigma * live).astype(BF16)
        slope = sigma * (1.0 + pre_act * (1.0 - sigma))
        grad_pre = (cotangent_ref[p].astype(F32) * slope * live).astype(BF16)
        half = jnp.zeros((outs, 64), BF16)
        wide = jnp.zeros((outs, 128), BF16)
        shifted = jnp.concatenate(
            [
                jnp.concatenate([grad_pre, wide], axis=1),
                jnp.concatenate([half, grad_pre, half], axis=1),
                jnp.concatenate([wide, grad_pre], axis=1),
            ],
            axis=0,
        )
        wsum[...] += jnp.dot(shifted, patches[...], preferred_element_type=F32)
        grad_patches[...] = lax.dot_general(
            shifted, weight, (((0,), (0,)), ((), ())), preferred_element_type=F32
        )

        for row in range(10):
            a, i = plane_of(row)

            def part(b, c):
                column = (3 * b + c) * 128
                return grad_patches[64 * row : 64 * row + 64, column : column + 128].reshape(8, 8, 128)

            def line_sum(c):
                return (
                    jnp.concatenate([part(0, c), blank, blank], axis=0)
                    + jnp.concatenate([blank, part(1, c), blank], axis=0)
                    + jnp.concatenate([blank, blank, part(2, c)], axis=0)
                )

            below = pltpu.roll(line_sum(0), 7, 1)
            above = pltpu.roll(line_sum(2), 1, 1)
            zero = jnp.zeros_like(below)
            middle = line_sum(1) + jnp.where(k == 7, zero, below) + jnp.where(k == 0, zero, above)
            for c, value in (
                (0, middle),
                (-1, jnp.where(k == 7, below, zero)),
                (1, jnp.where(k == 0, above, zero)),
            ):
                sums[slot[a, -1, c], i, 7:8] += value[0:1]
                sums[slot[a, 0, c], i] += value[1:9]
                sums[slot[a, 1, c], i, 0:1] += value[9:10]
        return carry

    lax.fori_loop(0, blocks, visit, 0)
    for slot in range(slots):
        grad_ref[slot] = sums[slot].reshape(512, 128).T.astype(BF16)
    rows = wsum.shape[0]
    for part in range(9):
        wgrad_ref[rows * part : rows * (part + 1)] = wsum[:, 128 * part : 128 * (part + 1)].astype(BF16)
    rest = wgrad_ref.shape[0] - 9 * rows
    if rest:
        wgrad_ref[9 * rows :] = jnp.zeros((rest, 128), BF16)


def reduce_kernel(
    space_count, with_weight, grad_ref, occupancy_ref, wgrad_ref, out_ref, wout_ref,
    near_buf, kept, passed, far_buf, rim_out, rim_in, wbuf,
    near_send, near_recv, far_send, far_recv, rim_send, rim_recv,
    scatter_send, scatter_recv, gather_send, gather_recv,
):
    blocks = out_ref.shape[0]
    s, c, before, after, near, far = places(space_count)
    peers = [lax.rem(s + d, space_count) for d in range(1, space_count)] if with_weight else [before, after]
    greet([(peer, c) for peer in peers] + [(s, near), (s, far)])

    def copy(source, target, send, recv, index, peer):
        return pltpu.make_async_remote_copy(
            src_ref=source,
            dst_ref=target,
            send_sem=send.at[index],
            recv_sem=recv.at[index],
            device_id=peer,
            device_id_type=MESH,
        )

    to_near = [
        copy(grad_ref.at[:, lax.rem(near, 2) + 2 * h], near_buf.at[h], near_send, near_recv, h, (s, near))
        for h in range(2)
    ]
    for each in to_near:
        each.start()
    scatters = []
    if with_weight:
        for d, peer in enumerate(peers):
            scatters.append(copy(wgrad_ref.at[peer], wbuf.at[d], scatter_send, scatter_recv, d, (peer, c)))
            scatters[-1].start()
    for each in to_near:
        each.wait_recv()
    mine, other = lax.div(c, 2), lax.div(far, 2)
    low, high = 0, blocks + 1
    own = pl.ds(1, blocks)
    to_far = [
        copy(passed.at[which], far_buf.at[which], far_send, far_recv, index, (s, far))
        for index, which in enumerate((low, high, own))
    ]
    for slots, sends in (((low, high), to_far[:2]), (range(1, blocks + 1), to_far[2:])):
        for slot in slots:
            passed[slot] = (grad_ref[slot, far].astype(F32) + near_buf[other, slot].astype(F32)).astype(BF16)
        for each in sends:
            each.start()
    for slot in range(blocks + 2):
        kept[slot] = grad_ref[slot, c].astype(F32) + near_buf[mine, slot].astype(F32)
    rims = []
    for index, (slot, peer) in enumerate(((low, before), (high, after))):
        to_far[index].wait_recv()
        rim_out[index] = (kept[slot] + far_buf[slot].astype(F32)).astype(BF16)
        rims.append(copy(rim_out.at[index], rim_in.at[index], rim_send, rim_recv, index, (peer, c)))
        rims[-1].start()
    to_far[2].wait_recv()
    for each in rims:
        each.wait_recv()
    for b in range(blocks):
        total = kept[1 + b] + far_buf[1 + b].astype(F32)
        if b == blocks - 1:
            total = total + rim_in[0].astype(F32)
        if b == 0:
            total = total + rim_in[1].astype(F32)
        out_ref[b] = (total * occupancy_ref[b : b + 1].astype(F32)).astype(BF16)
    if with_weight:
        total = wgrad_ref[s].astype(F32)
        for d, each in enumerate(scatters):
            each.wait_recv()
            total = total + wbuf[d].astype(F32)
        wout_ref[s] = total.astype(BF16)
        gathers = []
        for d, peer in enumerate(peers):
            gathers.append(copy(wout_ref.at[s], wout_ref.at[s], gather_send, gather_recv, d, (peer, c)))
            gathers[-1].start()
        for each in gathers:
            each.wait_recv()
        for each in scatters + gathers:
            each.wait_send()
    else:
        wout_ref[...] = wgrad_ref[...]
    for each in to_near + to_far + rims:
        each.wait_send()


def on_device(space_count, features, occupancy, weight, cotangent, neighbours):
    blocks, share = features.shape[:2]
    outs, _, cin = weight.shape
    slots = blocks + 2
    chans = cin // share
    with_weight = space_count <= 16
    vmem = pl.BlockSpec(memory_space=pltpu.VMEM)
    smem = pl.BlockSpec(memory_space=pltpu.SMEM)
    dma = pltpu.SemaphoreType.DMA

    full = pl.pallas_call(
        functools.partial(gather_kernel, space_count),
        out_shape=jax.ShapeDtypeStruct((slots, chans, share, 512), BF16),
        in_specs=[vmem] * 2,
        out_specs=vmem,
        scratch_shapes=[dma((11,)), dma((11,))],
        compiler_params=pltpu.CompilerParams(collective_id=0, has_side_effects=True),
        name="gather_blocks",
    )(features, occupancy)

    weight3 = jnp.transpose(weight.reshape(outs, 3, 9 * cin), (1, 0, 2)).reshape(3 * outs, 9 * cin)
    piece = -(-27 * outs // (16 * space_count)) * 16 if with_weight else 27 * outs // 4
    pieces = space_count if with_weight else 4
    act, grads, wgrad = pl.pallas_call(
        conv_kernel,
        out_shape=[
            jax.ShapeDtypeStruct(cotangent.shape, BF16),
            jax.ShapeDtypeStruct((slots, cin, 512), BF16),
            jax.ShapeDtypeStruct((pieces * piece, 128), BF16),
        ],
        in_specs=[smem] + [vmem] * 4,
        out_specs=[vmem] * 3,
        scratch_shapes=[
            pltpu.VMEM((slots + 1, 8, 8, 8, 128), F32),
            pltpu.VMEM((slots + 1, 8, 8, 8, 128), F32),
            pltpu.VMEM((640, 9 * cin), BF16),
            pltpu.VMEM((640, 9 * cin), F32),
            pltpu.VMEM((3 * outs, 9 * cin), F32),
        ],
        compiler_params=pltpu.CompilerParams(vmem_limit_bytes=48 * 2**20),
        name="conv_both_ways",
    )(
        neighbours,
        full.reshape(slots, cin, 512),
        occupancy.reshape(blocks, 1, 512),
        weight3,
        cotangent,
    )

    peers = pieces - 1
    grid = (slots, share, 512)
    input_grad, wtotal = pl.pallas_call(
        functools.partial(reduce_kernel, space_count, with_weight),
        out_shape=[
            jax.ShapeDtypeStruct((blocks, share, 512), BF16),
            jax.ShapeDtypeStruct((pieces, piece, 128), BF16),
        ],
        in_specs=[vmem] * 3,
        out_specs=[vmem] * 2,
        scratch_shapes=[
            pltpu.VMEM((2,) + grid, BF16),
            pltpu.VMEM(grid, F32),
            pltpu.VMEM(grid, BF16),
            pltpu.VMEM(grid, BF16),
            pltpu.VMEM((2, share, 512), BF16),
            pltpu.VMEM((2, share, 512), BF16),
            pltpu.VMEM((peers, piece, 128), BF16),
            dma((2,)), dma((2,)), dma((3,)), dma((3,)), dma((2,)), dma((2,)),
            dma((peers,)), dma((peers,)), dma((peers,)), dma((peers,)),
        ],
        compiler_params=pltpu.CompilerParams(
            collective_id=1, has_side_effects=True, vmem_limit_bytes=48 * 2**20
        ),
        name="reduce_grads",
    )(grads.reshape(slots, chans, share, 512), occupancy, wgrad.reshape(pieces, piece, 128))

    wflat = wtotal.reshape(pieces * piece, 128)[: 27 * outs].astype(F32)
    if not with_weight:
        wflat = lax.psum(wflat, "space")
    scaled = wflat * lax.rsqrt(F32(space_count * blocks * 512))
    weight_grad = jnp.transpose(scaled.reshape(9, 3, outs, cin), (2, 1, 0, 3)).reshape(outs, 27, cin)
    return (act, input_grad, weight_grad)


def solution(mesh):
    placed = (
        P("space", "chan", None),
        P("space", None),
        P("chan", None, None),
        P("space", "chan", None),
        P("space", None),
    )
    return jax.shard_map(
        functools.partial(on_device, mesh.shape["space"]),
        mesh=mesh,
        in_specs=placed,
        out_specs=(P("space", "chan", None), P("space", "chan", None), P("chan", None, None)),
        check_vma=False,
    )
```

time: 392 us -> 58.7 us (0.15)
  the two profiles are of different devices: /device:TPU:0 before, /device:TPU:29 now
where the time goes in v1:
time: 58.7 us; the launch traced here: 58.4 us
  Pallas kernels  51.9 us (88%)
  local copies, waits for them, and re-layouts  5.79 us (10%)
  between operations  0.71 us (1%)
    pallas_call x1, Pallas kernels, on_device(): pl.pallas_call(functools.partial(reduce_kernel, space_count, with_weight)...  27.7 us
    pallas_call x1, Pallas kernels, on_device(): pl.pallas_call(functools.partial(gather_kernel, space_count), out_shape=j...  13.8 us
    pallas_call x1, Pallas kernels, on_device(): pl.pallas_call(conv_kernel, out_shape=[jax.ShapeDtypeStruct(cotangent.sha...  10.3 us
    unnamed x10, local copies, waits for them, and re-layouts  3.8 us

profile of v1, /device:TPU:29, one launch (start us, length us, event | category | flops | bytes accessed | tf_op | source)
XLA Modules:
  0.0 58.4 jit_solution(4326207899488686719)
XLA Ops:
  0.6 0.7 %reshape.34.occupancy_ref = s32[4,1,512]{2,1,0:T(1,128)S(1)} reshape(s32[4,512]{1,0:T(4,128)} %occupancy_ref.3) | data formatting | bytes 16384 | tf_op jit(solution)/shard_map/reshape | solution.py:327
  1.3 1.3 %copy.9 = bf16[64,27,128]{2,1,0:T(8,128)(2,1)S(1)} copy(bf16[64,27,128]{2,0,1:T(8,128)(2,1)} %param.7) | data formatting | bytes 884736 | tf_op args[2]
  2.6 0.2 reshape.35
  2.9 0.0 copy-start.1
  2.9 0.0 copy-start.3
  3.0 13.8 %gather_blocks.1 = bf16[6,4,32,512]{3,2,1,0:T(8,128)(2,1)} custom-call(bf16[4,32,512]{2,1,0:T(8,128)(2,1)} %features_ref.1, s32[4,512]{1,0:T(4,128)} %occupancy_ref.3), custom_call_target="tpu_custom_call" | custom-call | tf_op jit(solution)/shard_map/gather_blocks/pallas_call | solution.py:293
  16.8 0.0 copy-done.1
  16.8 0.0 copy-done.3
  16.8 0.0 copy-start
  16.8 1.1 %copy-done = bf16[6,4,32,512]{3,2,1,0:T(8,128)(2,1)S(1)} copy-done((bf16[6,4,32,512]{3,2,1,0:T(8,128)(2,1)S(1)}, bf16[6,4,32,512]{3,2,1,0:T(8,128)(2,1)}, u32[]{:S(2)}) %copy-start) | copy-done | bytes 786456
  18.0 10.3 %conv_both_ways.1 = (bf16[4,64,512]{2,1,0:T(8,128)(2,1)}, bf16[6,128,512]{2,1,0:T(8,128)(2,1)S(1)}, bf16[1792,128]{1,0:T(8,128)(2,1)S(1)}) custom-call(s32[4,26]{1,0:T(4,128)S(1)} %copy-done.3, bf16[6,128,512]{2,1,0:T(8,128)(2,1)S(1)} %bitcast.10, s32[4,1,512]{2,1,0:T(1,128)S(1)} %reshape.34.occupancy_ref, bf16[192,1152]{1,0:T(8,128)(2,1)S(1)} %bitcast.11, ...), custom_call_target="tpu_custom_call" | custom-call | tf_op jit(solution)/shard_map/conv_both_ways/pallas_call | solution.py:306
  28.3 0.0 copy-start.2
  28.3 0.7 %copy-done.2 = s32[4,512]{1,0:T(4,128)S(1)} copy-done((s32[4,512]{1,0:T(4,128)S(1)}, s32[4,512]{1,0:T(4,128)}, u32[]{:S(2)}) %copy-start.2) | copy-done | bytes 8216
  29.0 27.7 %reduce_grads.1 = (bf16[4,32,512]{2,1,0:T(8,128)(2,1)S(1)}, bf16[8,224,128]{2,1,0:T(8,128)(2,1)S(1)}) custom-call(bf16[6,4,32,512]{3,2,1,0:T(8,128)(2,1)S(1)} %bitcast.12, s32[4,512]{1,0:T(4,128)S(1)} %copy-done.2, bf16[8,224,128]{2,1,0:T(8,128)(2,1)S(1)} %bitcast.13), custom_call_target="tpu_custom_call" | custom-call | tf_op jit(solution)/shard_map/reduce_grads/pallas_call | solution.py:334
  56.7 0.1 convert_multiply_fusion
  56.8 1.0 %copy.11 = f32[9,3,64,128]{3,2,0,1:T(8,128)} copy(f32[9,3,64,128]{3,2,1,0:T(8,128)S(1)} %bitcast.15) | data formatting | bytes 1769472 | tf_op jit(solution)/shard_map/reshape | solution.py:363
  57.8 0.7 %copy.13 = bf16[4,32,512]{2,1,0:T(8,128)(2,1)} copy(bf16[4,32,512]{2,1,0:T(8,128)(2,1)S(1)} %get-tuple-element.17) | data formatting | bytes 262144
  (1 shorter events, 0.0 us)
Async XLA Ops:
  2.9 13.9 %copy-start.1 = (bf16[4,64,512]{2,1,0:T(8,128)(2,1)S(1)}, bf16[4,64,512]{2,1,0:T(8,128)(2,1)}, u32[]{:S(2)}) copy-start(bf16[4,64,512]{2,1,0:T(8,128)(2,1)} %cotangent_ref.1) | copy-start | bytes 786436
  2.9 13.9 %copy-start.3 = (s32[4,26]{1,0:T(4,128)S(1)}, s32[4,26]{1,0:T(4,128)}, u32[]{:S(2)}) copy-start(s32[4,26]{1,0:T(4,128)} %neighbours_ref.1) | copy-start | bytes 1252
  16.8 1.1 %copy-start = (bf16[6,4,32,512]{3,2,1,0:T(8,128)(2,1)S(1)}, bf16[6,4,32,512]{3,2,1,0:T(8,128)(2,1)}, u32[]{:S(2)}) copy-start(bf16[6,4,32,512]{3,2,1,0:T(8,128)(2,1)} %gather_blocks.1) | copy-start | bytes 2359300
  28.3 0.7 %copy-start.2 = (s32[4,512]{1,0:T(4,128)S(1)}, s32[4,512]{1,0:T(4,128)}, u32[]{:S(2)}) copy-start(s32[4,512]{1,0:T(4,128)} %occupancy_ref.3) | copy-start | bytes 24580

commit v2 on v1

v2 whole, which is shorter than its diff:
```python
import functools

import jax
import jax.numpy as jnp
from jax import lax
from jax.experimental import pallas as pl
from jax.experimental.pallas import tpu as pltpu
from jax.sharding import PartitionSpec as P

MESH = pl.DeviceIdType.MESH
F32 = jnp.float32
BF16 = jnp.bfloat16


def places(space_count):
    s, c = lax.axis_index("space"), lax.axis_index("chan")
    before = lax.rem(s + space_count - 1, space_count)
    after = lax.rem(s + 1, space_count)
    near = c + 1 - 2 * lax.rem(c, 2)
    far = lax.rem(c + 2, 4)
    return s, c, before, after, near, far


def greet(peers):
    barrier = pltpu.get_barrier_semaphore()
    for peer in peers:
        pl.semaphore_signal(barrier, inc=1, device_id=peer, device_id_type=MESH)
    pl.semaphore_wait(barrier, len(peers))


def whole_kernel(
    space_count, with_weight,
    neighbours_ref, features_ref, occupancy_ref, weight_ref, cotangent_ref,
    act_ref, out_ref, wout_ref,
    full, cubes, sums, patches, grad_patches, shifted, wsum,
    wsend, ybuf, zsend, zbuf, wown, grads, near_buf, kept, passed, far_buf, rim_out, rim_in,
    load_send, load_recv, near_send, near_recv, far_send, far_recv, rim_send, rim_recv,
    y_send, y_recv, z_send, z_recv, zg_send, zg_recv, yg_send, yg_recv,
):
    blocks, share = features_ref.shape[:2]
    outs = cotangent_ref.shape[1]
    slots = blocks + 2
    s, c, before, after, near, far = places(space_count)
    y = lax.rem(s, 2)
    z = lax.div(s, 2)
    beside = s + 1 - 2 * y

    def copy(source, target, send, recv, index, peer):
        return pltpu.make_async_remote_copy(
            src_ref=source,
            dst_ref=target,
            send_sem=send.at[index],
            recv_sem=recv.at[index],
            device_id=peer,
            device_id_type=MESH,
        )

    peers = [(before, c), (after, c), (s, near), (s, far)]
    if with_weight:
        peers += [(lax.rem(s + 2 * d, space_count), c) for d in range(1, 4)]
    greet(peers)

    def spread(slots_from, piece, slots_to, peer, index):
        return copy(full.at[slots_from, piece], full.at[slots_to, piece], load_send, load_recv, index, peer)

    own = pl.ds(1, blocks)
    low, high = 0, blocks + 1
    for b in (0, blocks - 1, *range(1, blocks - 1)):
        mask = occupancy_ref[b : b + 1].astype(F32)
        full[1 + b, c] = (features_ref[b].astype(F32) * mask).astype(BF16)
    rim_down = spread(1, c, high, (before, c), 0)
    rim_up = spread(blocks, c, low, (after, c), 1)
    own_far = spread(own, c, own, (s, far), 2)
    own_near = spread(own, c, own, (s, near), 3)
    high_far = spread(high, c, high, (s, far), 4)
    low_far = spread(low, c, low, (s, far), 5)
    high_near = spread(high, c, high, (s, near), 6)
    low_near = spread(low, c, low, (s, near), 7)
    own_pass = spread(own, far, own, (s, near), 8)
    high_pass = spread(high, far, high, (s, near), 9)
    low_pass = spread(low, far, low, (s, near), 10)
    for each in (rim_down, rim_up, own_far, own_near):
        each.start()
    cubes[slots] = jnp.zeros((8, 8, 8, 128), F32)
    sums[...] = jnp.zeros(sums.shape, F32)
    wsum[...] = jnp.zeros(wsum.shape, F32)
    shifted[...] = jnp.zeros(shifted.shape, BF16)
    k = lax.broadcasted_iota(jnp.int32, (10, 8, 128), 1)
    blank = jnp.zeros((1, 8, 128), F32)
    own_far.wait_recv()
    own_pass.start()
    rim_down.wait_recv()
    rim_up.wait_recv()
    for each in (high_far, low_far, high_near, low_near):
        each.start()

    def turn(slot):
        cubes[slot] = full[slot].reshape(4 * share, 512).astype(F32).T.reshape(8, 8, 8, 128)

    own_near.wait_recv()
    own_pass.wait_recv()
    for slot in range(1, blocks + 1):
        turn(slot)

    def plane_of(row):
        a = -1 if row == 0 else (1 if row == 9 else 0)
        return a, (row - 1) % 8

    def offsets():
        for number in range(27):
            yield number, (number // 9 - 1, number // 3 % 3 - 1, number % 3 - 1)

    def forward(t, carry):
        p = lax.rem(t + 1, blocks)

        @pl.when(t == blocks - 2)
        def _():
            high_far.wait_recv()
            low_far.wait_recv()
            high_pass.start()
            low_pass.start()
            for each in (high_near, low_near, high_pass, low_pass):
                each.wait_recv()
            turn(low)
            turn(high)

        slot = {}
        for number, offset in offsets():
            if number == 13:
                slot[offset] = p + 1
            else:
                named = neighbours_ref[p, number - (number > 13)]
                near_id = jnp.clip(named - s * blocks + 1, 0, slots)
                slot[offset] = jnp.where(named < 0, slots, near_id)

        for row in range(10):
            a, i = plane_of(row)

            def line(c):
                return jnp.concatenate(
                    [cubes[slot[a, -1, c], i, 7:8], cubes[slot[a, 0, c], i], cubes[slot[a, 1, c], i, 0:1]],
                    axis=0,
                )

            middle = line(0)
            views = (
                pltpu.roll(jnp.where(k == 7, line(-1), middle), 1, 1),
                middle,
                pltpu.roll(jnp.where(k == 0, line(1), middle), 7, 1),
            )
            for b in range(3):
                for c in range(3):
                    piece = views[c][b : b + 8].reshape(64, 128).astype(BF16)
                    patches[64 * row : 64 * row + 64, (3 * b + c) * 128 : (3 * b + c + 1) * 128] = piece

        product = lax.dot_general(
            weight_ref[...], patches[...], (((1,), (1,)), ((), ())), preferred_element_type=F32
        )
        pre_act = (
            product[:outs, 0:512] + product[outs : 2 * outs, 64:576] + product[2 * outs :, 128:640]
        )
        live = occupancy_ref[pl.ds(p, 1)].astype(F32)
        sigma = jax.nn.sigmoid(pre_act)
        act_ref[p] = (pre_act * sigma * live).astype(BF16)
        slope = sigma * (1.0 + pre_act * (1.0 - sigma))
        grad_pre = (cotangent_ref[p].astype(F32) * slope * live).astype(BF16)
        half = jnp.zeros((outs, 64), BF16)
        shifted[p, :outs, 0:512] = grad_pre
        shifted[p, outs : 2 * outs] = jnp.concatenate([half, grad_pre, half], axis=1)
        shifted[p, 2 * outs :, 128:640] = grad_pre
        wsum[...] += jnp.dot(shifted[p], patches[...], preferred_element_type=F32)
        return carry

    lax.fori_loop(0, blocks, forward, 0)

    rows = wsum.shape[0]
    for part in range(9):
        wsend[rows * part : rows * (part + 1)] = wsum[:, 128 * part : 128 * (part + 1)].astype(BF16)
    rest = wsend.shape[0] - 9 * rows
    if rest:
        wsend[9 * rows :] = jnp.zeros((rest, 128), BF16)
    height = ybuf.shape[1]

    def cut(parity, place):
        return pl.ds(pl.multiple_of((parity * 4 + place) * height, 16), height)

    def to_beside(j):
        place = lax.rem(z + 1 + j, 4)
        return copy(wsend.at[cut(1 - y, place)], ybuf.at[place], y_send, y_recv, j, (beside, c))

    def to_level(j):
        place = lax.rem(z + 1 + j, 4)
        return copy(zsend.at[j], zbuf.at[j], z_send, z_recv, j, (2 * place + y, c))

    if with_weight:
        for j in range(4):
            to_beside(j).start()

    def backward(p, carry):
        grad_patches[...] = lax.dot_general(
            shifted[p], weight_ref[...], (((0,), (0,)), ((), ())), preferred_element_type=F32
        )
        share_of = {}
        for number, offset in offsets():
            if number == 13:
                named = s * blocks + p
            else:
                named = neighbours_ref[p, number - (number > 13)]
                named = jnp.where(named < 0, -9, named)
            for q in range(slots):
                share_of[q, offset] = jnp.where(named == s * blocks - 1 + q, 1.0, 0.0).astype(F32)

        for row in range(10):
            a, i = plane_of(row)

            def part(b, c):
                column = (3 * b + c) * 128
                return grad_patches[64 * row : 64 * row + 64, column : column + 128].reshape(8, 8, 128)

            def line_sum(c):
                return (
                    jnp.concatenate([part(0, c), blank, blank], axis=0)
                    + jnp.concatenate([blank, part(1, c), blank], axis=0)
                    + jnp.concatenate([blank, blank, part(2, c)], axis=0)
                )

            below = pltpu.roll(line_sum(0), 7, 1)
            above = pltpu.roll(line_sum(2), 1, 1)
            zero = jnp.zeros_like(below)
            middle = line_sum(1) + jnp.where(k == 7, zero, below) + jnp.where(k == 0, zero, above)
            values = (jnp.where(k == 7, below, zero), middle, jnp.where(k == 0, above, zero))
            for q in range(slots):

                def weighed(b, first, last):
                    return sum(share_of[q, (a, b, c - 1)] * values[c][first:last] for c in range(3))

                delta = weighed(0, 1, 9)
                delta = jnp.concatenate(
                    [delta[0:1] + weighed(1, 9, 10), delta[1:7], delta[7:8] + weighed(-1, 0, 1)], axis=0
                )
                sums[q, i] = sums[q, i] + delta

        if with_weight:
            to_beside(p).wait_recv()
            place = lax.rem(z + 1 + p, 4)
            joined = wsend[cut(y, place)].astype(F32) + ybuf[place].astype(F32)

            @pl.when(p < 3)
            def _():
                zsend[p] = joined.astype(BF16)
                to_level(p).start()

            @pl.when(p == 3)
            def _():
                wown[...] = joined

        return carry

    lax.fori_loop(0, blocks, backward, 0)

    for slot in range(slots):
        grads[slot] = sums[slot].reshape(512, 128).T.astype(BF16).reshape(4, share, 512)
    to_near = [
        copy(grads.at[:, lax.rem(near, 2) + 2 * h], near_buf.at[h], near_send, near_recv, h, (s, near))
        for h in range(2)
    ]
    for each in to_near:
        each.start()
    sent = [
        rim_down, rim_up, own_far, own_near, high_far, low_far,
        high_near, low_near, own_pass, high_pass, low_pass,
    ] + to_near
    if with_weight:
        total = wown[...]
        for j in range(3):
            to_level(j).wait_recv()
            total = total + zbuf[j].astype(F32)
        wout_ref[cut(y, z)] = total.astype(BF16)
        mine = wout_ref.at[cut(y, z)]
        levels = [
            copy(mine, mine, zg_send, zg_recv, j, (2 * lax.rem(z + 1 + j, 4) + y, c)) for j in range(3)
        ]
        asides = []
        for j in range(4):
            piece = wout_ref.at[cut(y, lax.rem(z + 4 - j, 4))]
            asides.append(copy(piece, piece, yg_send, yg_recv, j, (beside, c)))
        for each in levels + asides[:1]:
            each.start()
        sent += levels + asides + [to_beside(j) for j in range(4)] + [to_level(j) for j in range(3)]
    else:
        wout_ref[...] = wsend[...]

    for each in to_near:
        each.wait_recv()
    kin, other = lax.div(c, 2), lax.div(far, 2)
    to_far = [
        copy(passed.at[which], far_buf.at[which], far_send, far_recv, index, (s, far))
        for index, which in enumerate((low, high, own))
    ]
    for group, sends in (((low, high), to_far[:2]), (range(1, blocks + 1), to_far[2:])):
        for slot in group:
            passed[slot] = (grads[slot, far].astype(F32) + near_buf[other, slot].astype(F32)).astype(BF16)
        for each in sends:
            each.start()
    for slot in range(slots):
        kept[slot] = grads[slot, c].astype(F32) + near_buf[kin, slot].astype(F32)
    rims = []
    for index, (slot, peer) in enumerate(((low, before), (high, after))):
        to_far[index].wait_recv()
        rim_out[index] = (kept[slot] + far_buf[slot].astype(F32)).astype(BF16)
        rims.append(copy(rim_out.at[index], rim_in.at[index], rim_send, rim_recv, index, (peer, c)))
        rims[-1].start()
    sent += to_far + rims
    if with_weight:
        for j in range(3):
            levels[j].wait_recv()
            asides[j + 1].start()
    to_far[2].wait_recv()
    for each in rims:
        each.wait_recv()
    for b in range(blocks):
        total = kept[1 + b] + far_buf[1 + b].astype(F32)
        if b == blocks - 1:
            total = total + rim_in[0].astype(F32)
        if b == 0:
            total = total + rim_in[1].astype(F32)
        out_ref[b] = (total * occupancy_ref[b : b + 1].astype(F32)).astype(BF16)
    if with_weight:
        for each in asides:
            each.wait_recv()
    for each in sent:
        each.wait_send()


def on_device(space_count, features, occupancy, weight, cotangent, neighbours):
    blocks, share = features.shape[:2]
    outs, _, cin = weight.shape
    slots = blocks + 2
    with_weight = space_count == 8 and blocks == 4
    height = -(-27 * outs // 128) * 16
    vmem = pl.BlockSpec(memory_space=pltpu.VMEM)
    smem = pl.BlockSpec(memory_space=pltpu.SMEM)
    dma = pltpu.SemaphoreType.DMA
    weight3 = jnp.transpose(weight.reshape(outs, 3, 9 * cin), (1, 0, 2)).reshape(3 * outs, 9 * cin)
    grid = (slots, share, 512)
    act, input_grad, wtotal = pl.pallas_call(
        functools.partial(whole_kernel, space_count, with_weight),
        out_shape=[
            jax.ShapeDtypeStruct(cotangent.shape, BF16),
            jax.ShapeDtypeStruct((blocks, share, 512), BF16),
            jax.ShapeDtypeStruct((8 * height, 128), BF16),
        ],
        in_specs=[smem] + [vmem] * 4,
        out_specs=[vmem] * 3,
        scratch_shapes=[
            pltpu.VMEM((slots, 4, share, 512), BF16),
            pltpu.VMEM((slots + 1, 8, 8, 8, 128), F32),
            pltpu.VMEM((slots, 8, 8, 8, 128), F32),
            pltpu.VMEM((640, 9 * cin), BF16),
            pltpu.VMEM((640, 9 * cin), F32),
            pltpu.VMEM((blocks, 3 * outs, 640), BF16),
            pltpu.VMEM((3 * outs, 9 * cin), F32),
            pltpu.VMEM((8 * height, 128), BF16),
            pltpu.VMEM((4, height, 128), BF16),
            pltpu.VMEM((3, height, 128), BF16),
            pltpu.VMEM((3, height, 128), BF16),
            pltpu.VMEM((height, 128), F32),
            pltpu.VMEM((slots, 4, share, 512), BF16),
            pltpu.VMEM((2,) + grid, BF16),
            pltpu.VMEM(grid, F32),
            pltpu.VMEM(grid, BF16),
            pltpu.VMEM(grid, BF16),
            pltpu.VMEM((2, share, 512), BF16),
            pltpu.VMEM((2, share, 512), BF16),
        ]
        + [dma((n,)) for n in (11, 11, 2, 2, 3, 3, 2, 2, 4, 4, 3, 3, 3, 3, 4, 4)],
        compiler_params=pltpu.CompilerParams(
            collective_id=0, has_side_effects=True, vmem_limit_bytes=48 * 2**20
        ),
        name="conv_both_ways",
    )(neighbours, features, occupancy, weight3, cotangent)

    wflat = wtotal[: 27 * outs].astype(F32)
    if not with_weight:
        wflat = lax.psum(wflat, "space")
    scaled = wflat * lax.rsqrt(F32(space_count * blocks * 512))
    weight_grad = jnp.transpose(scaled.reshape(9, 3, outs, cin), (2, 1, 0, 3)).reshape(outs, 27, cin)
    return (act, input_grad, weight_grad)


def solution(mesh):
    placed = (
        P("space", "chan", None),
        P("space", None),
        P("chan", None, None),
        P("space", "chan", None),
        P("space", None),
    )
    return jax.shard_map(
        functools.partial(on_device, mesh.shape["space"]),
        mesh=mesh,
        in_specs=placed,
        out_specs=(P("space", "chan", None), P("space", "chan", None), P("chan", None, None)),
        check_vma=False,
    )
```

time: 58.7 us -> 45.7 us (0.78)
  the two profiles are of different devices: /device:TPU:29 before, /device:TPU:0 now
where the time goes in v2:
time: 45.7 us; the launch traced here: 45.5 us
  Pallas kernels  39.9 us (87%)
  local copies, waits for them, and re-layouts  4.85 us (11%)
  between operations  0.7 us (2%)
    pallas_call x1, Pallas kernels, on_device(): pl.pallas_call(functools.partial(whole_kernel, space_count, with_weight),...  39.9 us
    unnamed x11, local copies, waits for them, and re-layouts  3.57 us
    transpose x1, local copies, waits for them, and re-layouts, on_device(): jnp.transpose(scaled.reshape(9, 3, outs, cin), (2, 1, 0, 3))  1.01 us

profile of v2, /device:TPU:0, one launch (start us, length us, event | category | flops | bytes accessed | tf_op | source)
XLA Modules:
  0.0 45.5 jit_solution(12407075253661511277)
XLA Ops:
  0.6 1.3 %copy.9 = bf16[64,27,128]{2,1,0:T(8,128)(2,1)S(1)} copy(bf16[64,27,128]{2,0,1:T(8,128)(2,1)} %param.7) | data formatting | bytes 884736 | tf_op args[2]
  1.9 0.2 reshape.18
  2.2 0.0 copy-start
  2.2 0.0 copy-start.1
  2.2 0.0 copy-start.2
  2.2 0.0 copy-start.3
  2.3 0.8 %copy-done = bf16[4,64,512]{2,1,0:T(8,128)(2,1)S(1)} copy-done((bf16[4,64,512]{2,1,0:T(8,128)(2,1)S(1)}, bf16[4,64,512]{2,1,0:T(8,128)(2,1)}, u32[]{:S(2)}) %copy-start) | copy-done | bytes 262168
  3.1 0.0 copy-done.1
  3.2 0.0 copy-done.2
  3.2 0.0 copy-done.3
  3.2 39.9 %conv_both_ways.1 = (bf16[4,64,512]{2,1,0:T(8,128)(2,1)S(1)}, bf16[4,32,512]{2,1,0:T(8,128)(2,1)S(1)}, bf16[1792,128]{1,0:T(8,128)(2,1)S(1)}) custom-call(s32[4,26]{1,0:T(4,128)S(1)} %copy-done.3, bf16[4,32,512]{2,1,0:T(8,128)(2,1)S(1)} %copy-done.1, s32[4,512]{1,0:T(4,128)S(1)} %copy-done.2, bf16[192,1152]{1,0:T(8,128)(2,1)S(1)} %bitcast.6, ...), custom_call_target="tpu_custom_call" | custom-call | tf_op jit(solution)/shard_map/conv_both_ways/pallas_call | solution.py:346
  43.1 0.1 convert_multiply_fusion
  43.1 1.0 %copy.11 = f32[64,3,9,128]{3,0,2,1:T(8,128)} copy(f32[64,3,9,128]{3,0,1,2:T(8,128)S(1)} %bitcast.7) | data formatting | bytes 1769472 | tf_op jit(solution)/shard_map/transpose | solution.py:387
  44.1 0.7 %copy.14 = bf16[4,64,512]{2,1,0:T(8,128)(2,1)} copy(bf16[4,64,512]{2,1,0:T(8,128)(2,1)S(1)} %get-tuple-element.12) | data formatting | bytes 524288
  44.8 0.7 %copy.15 = bf16[4,32,512]{2,1,0:T(8,128)(2,1)} copy(bf16[4,32,512]{2,1,0:T(8,128)(2,1)S(1)} %get-tuple-element.13) | data formatting | bytes 262144
  (1 shorter events, 0.0 us)
Async XLA Ops:
  2.2 1.0 %copy-start = (bf16[4,64,512]{2,1,0:T(8,128)(2,1)S(1)}, bf16[4,64,512]{2,1,0:T(8,128)(2,1)}, u32[]{:S(2)}) copy-start(bf16[4,64,512]{2,1,0:T(8,128)(2,1)} %cotangent_ref.1) | copy-start | bytes 786436
  2.2 1.0 %copy-start.1 = (bf16[4,32,512]{2,1,0:T(8,128)(2,1)S(1)}, bf16[4,32,512]{2,1,0:T(8,128)(2,1)}, u32[]{:S(2)}) copy-start(bf16[4,32,512]{2,1,0:T(8,128)(2,1)} %features_ref.1) | copy-start | bytes 393220
  2.2 1.0 %copy-start.2 = (s32[4,512]{1,0:T(4,128)S(1)}, s32[4,512]{1,0:T(4,128)}, u32[]{:S(2)}) copy-start(s32[4,512]{1,0:T(4,128)} %occupancy_ref.1) | copy-start | bytes 24580
  2.2 1.0 %copy-start.3 = (s32[4,26]{1,0:T(4,128)S(1)}, s32[4,26]{1,0:T(4,128)}, u32[]{:S(2)}) copy-start(s32[4,26]{1,0:T(4,128)} %neighbours_ref.1) | copy-start | bytes 1252

commit v3 on v2

--- a/solution.py
+++ b/solution.py
@@ -30,16 +30,22 @@
 
 def whole_kernel(
     space_count, with_weight,
-    neighbours_ref, features_ref, occupancy_ref, weight_ref, cotangent_ref,
+    neighbours_ref, features_ref, occupancy_ref, weight_hbm, cotangent_hbm,
     act_ref, out_ref, wout_ref,
-    full, cubes, sums, patches, grad_patches, shifted, wsum,
+    weight_ref, cotangent_ref, full, cubes, sums, patches, grad_patches, shifted, wsum,
     wsend, ybuf, zsend, zbuf, wown, grads, near_buf, kept, passed, far_buf, rim_out, rim_in,
-    load_send, load_recv, near_send, near_recv, far_send, far_recv, rim_send, rim_recv,
+    fetch, load_send, load_recv, near_send, near_recv, far_send, far_recv, rim_send, rim_recv,
     y_send, y_recv, z_send, z_recv, zg_send, zg_recv, yg_send, yg_recv,
 ):
     blocks, share = features_ref.shape[:2]
     outs = cotangent_ref.shape[1]
     slots = blocks + 2
+    fetches = [pltpu.make_async_copy(cotangent_hbm, cotangent_ref, fetch.at[27])]
+    for n in range(27):
+        rows, columns = pl.ds(n // 9 * outs, outs), pl.ds(n % 9 * 128, 128)
+        fetches.append(pltpu.make_async_copy(weight_hbm.at[n], weight_ref.at[rows, columns], fetch.at[n]))
+    for each in fetches:
+        each.start()
     s, c, before, after, near, far = places(space_count)
     y = lax.rem(s, 2)
     z = lax.div(s, 2)
@@ -97,6 +103,8 @@
     def turn(slot):
         cubes[slot] = full[slot].reshape(4 * share, 512).astype(F32).T.reshape(8, 8, 8, 128)
 
+    for each in fetches:
+        each.wait()
     own_near.wait_recv()
     own_pass.wait_recv()
     for slot in range(1, blocks + 1):
@@ -173,12 +181,12 @@
 
     lax.fori_loop(0, blocks, forward, 0)
 
-    rows = wsum.shape[0]
-    for part in range(9):
-        wsend[rows * part : rows * (part + 1)] = wsum[:, 128 * part : 128 * (part + 1)].astype(BF16)
-    rest = wsend.shape[0] - 9 * rows
+    for n in range(27):
+        part = wsum[n // 9 * outs : (n // 9 + 1) * outs, n % 9 * 128 : (n % 9 + 1) * 128]
+        wsend[outs * n : outs * (n + 1)] = part.astype(BF16)
+    rest = wsend.shape[0] - 27 * outs
     if rest:
-        wsend[9 * rows :] = jnp.zeros((rest, 128), BF16)
+        wsend[27 * outs :] = jnp.zeros((rest, 128), BF16)
     height = ybuf.shape[1]
 
     def cut(parity, place):
@@ -196,7 +204,10 @@
         for j in range(4):
             to_beside(j).start()
 
-    def backward(p, carry):
+    def targets(rim):
+        return [*range(1, blocks + 1), *([] if rim is None else [rim])]
+
+    def backward(p, j, rim):
         grad_patches[...] = lax.dot_general(
             shifted[p], weight_ref[...], (((0,), (0,)), ((), ())), preferred_element_type=F32
         )
@@ -207,8 +218,8 @@
             else:
                 named = neighbours_ref[p, number - (number > 13)]
                 named = jnp.where(named < 0, -9, named)
-            for q in range(slots):
-                share_of[q, offset] = jnp.where(named == s * blocks - 1 + q, 1.0, 0.0).astype(F32)
+            for index, q in enumerate(targets(rim)):
+                share_of[index, offset] = jnp.where(named == s * blocks - 1 + q, 1.0, 0.0).astype(F32)
 
         for row in range(10):
             a, i = plane_of(row)
@@ -229,10 +240,10 @@
             zero = jnp.zeros_like(below)
             middle = line_sum(1) + jnp.where(k == 7, zero, below) + jnp.where(k == 0, zero, above)
             values = (jnp.where(k == 7, below, zero), middle, jnp.where(k == 0, above, zero))
-            for q in range(slots):
+            for index, q in enumerate(targets(rim)):
 
                 def weighed(b, first, last):
-                    return sum(share_of[q, (a, b, c - 1)] * values[c][first:last] for c in range(3))
+                    return sum(share_of[index, (a, b, c - 1)] * values[c][first:last] for c in range(3))
 
                 delta = weighed(0, 1, 9)
                 delta = jnp.concatenate(
@@ -241,35 +252,76 @@
                 sums[q, i] = sums[q, i] + delta
 
         if with_weight:
-            to_beside(p).wait_recv()
-            place = lax.rem(z + 1 + p, 4)
+            to_beside(j).wait_recv()
+            place = lax.rem(z + 1 + j, 4)
             joined = wsend[cut(y, place)].astype(F32) + ybuf[place].astype(F32)
 
-            @pl.when(p < 3)
+            @pl.when(j < 3)
             def _():
-                zsend[p] = joined.astype(BF16)
-                to_level(p).start()
-
-            @pl.when(p == 3)
+                zsend[j] = joined.astype(BF16)
+                to_level(j).start()
+
+            @pl.when(j == 3)
             def _():
                 wown[...] = joined
 
-        return carry
-
-    lax.fori_loop(0, blocks, backward, 0)
-
-    for slot in range(slots):
-        grads[slot] = sums[slot].reshape(512, 128).T.astype(BF16).reshape(4, share, 512)
+    kin, other = lax.div(c, 2), lax.div(far, 2)
+    parts = (low, high, own)
     to_near = [
-        copy(grads.at[:, lax.rem(near, 2) + 2 * h], near_buf.at[h], near_send, near_recv, h, (s, near))
+        copy(
+            grads.at[which, lax.rem(near, 2) + 2 * h], near_buf.at[h, which],
+            near_send, near_recv, 2 * index + h, (s, near),
+        )
+        for index, which in enumerate(parts)
         for h in range(2)
     ]
-    for each in to_near:
-        each.start()
+    to_far = [
+        copy(passed.at[which], far_buf.at[which], far_send, far_recv, index, (s, far))
+        for index, which in enumerate(parts)
+    ]
+    rims = [
+        copy(rim_out.at[index], rim_in.at[index], rim_send, rim_recv, index, (peer, c))
+        for index, peer in enumerate((before, after))
+    ]
     sent = [
         rim_down, rim_up, own_far, own_near, high_far, low_far,
         high_near, low_near, own_pass, high_pass, low_pass,
-    ] + to_near
+    ] + to_near + to_far + rims
+
+    def flip(slot):
+        grads[slot] = sums[slot].reshape(512, 128).T.astype(BF16).reshape(4, share, 512)
+
+    def merge_near(slot):
+        passed[slot] = (grads[slot, far].astype(F32) + near_buf[other, slot].astype(F32)).astype(BF16)
+        kept[slot] = grads[slot, c].astype(F32) + near_buf[kin, slot].astype(F32)
+
+    def edges(t, carry):
+        backward(t * (blocks - 1), t, t * (blocks + 1))
+        return carry
+
+    def inner(p, carry):
+        @pl.when(p == blocks - 2)
+        def _():
+            for each in to_near[:4]:
+                each.wait_recv()
+            for index, slot in enumerate((low, high)):
+                merge_near(slot)
+                to_far[index].start()
+
+        backward(p, p + 1, None)
+        return carry
+
+    lax.fori_loop(0, 2, edges, 0)
+    flip(low)
+    flip(high)
+    for each in to_near[:4]:
+        each.start()
+    lax.fori_loop(1, blocks - 1, inner, 0)
+
+    for slot in range(1, blocks + 1):
+        flip(slot)
+    for each in to_near[4:]:
+        each.start()
     if with_weight:
         total = wown[...]
         for j in range(3):
@@ -290,27 +342,15 @@
     else:
         wout_ref[...] = wsend[...]
 
-    for each in to_near:
-        each.wait_recv()
-    kin, other = lax.div(c, 2), lax.div(far, 2)
-    to_far = [
-        copy(passed.at[which], far_buf.at[which], far_send, far_recv, index, (s, far))
-        for index, which in enumerate((low, high, own))
-    ]
-    for group, sends in (((low, high), to_far[:2]), (range(1, blocks + 1), to_far[2:])):
-        for slot in group:
-            passed[slot] = (grads[slot, far].astype(F32) + near_buf[other, slot].astype(F32)).astype(BF16)
-        for each in sends:
-            each.start()
-    for slot in range(slots):
-        kept[slot] = grads[slot, c].astype(F32) + near_buf[kin, slot].astype(F32)
-    rims = []
-    for index, (slot, peer) in enumerate(((low, before), (high, after))):
+    for index, slot in enumerate((low, high)):
         to_far[index].wait_recv()
         rim_out[index] = (kept[slot] + far_buf[slot].astype(F32)).astype(BF16)
-        rims.append(copy(rim_out.at[index], rim_in.at[index], rim_send, rim_recv, index, (peer, c)))
-        rims[-1].start()
-    sent += to_far + rims
+        rims[index].start()
+    for each in to_near[4:]:
+        each.wait_recv()
+    for slot in range(1, blocks + 1):
+        merge_near(slot)
+    to_far[2].start()
     if with_weight:
         for j in range(3):
             levels[j].wait_recv()
@@ -341,7 +381,6 @@
     vmem = pl.BlockSpec(memory_space=pltpu.VMEM)
     smem = pl.BlockSpec(memory_space=pltpu.SMEM)
     dma = pltpu.SemaphoreType.DMA
-    weight3 = jnp.transpose(weight.reshape(outs, 3, 9 * cin), (1, 0, 2)).reshape(3 * outs, 9 * cin)
     grid = (slots, share, 512)
     act, input_grad, wtotal = pl.pallas_call(
         functools.partial(whole_kernel, space_count, with_weight),
@@ -350,9 +389,11 @@
             jax.ShapeDtypeStruct((blocks, share, 512), BF16),
             jax.ShapeDtypeStruct((8 * height, 128), BF16),
         ],
-        in_specs=[smem] + [vmem] * 4,
+        in_specs=[smem] + [vmem] * 2 + [pl.BlockSpec(memory_space=pl.ANY)] * 2,
         out_specs=[vmem] * 3,
         scratch_shapes=[
+            pltpu.VMEM((3 * outs, 9 * cin), BF16),
+            pltpu.VMEM(cotangent.shape, BF16),
             pltpu.VMEM((slots, 4, share, 512), BF16),
             pltpu.VMEM((slots + 1, 8, 8, 8, 128), F32),
             pltpu.VMEM((slots, 8, 8, 8, 128), F32),
@@ -373,18 +414,18 @@
             pltpu.VMEM((2, share, 512), BF16),
             pltpu.VMEM((2, share, 512), BF16),
         ]
-        + [dma((n,)) for n in (11, 11, 2, 2, 3, 3, 2, 2, 4, 4, 3, 3, 3, 3, 4, 4)],
+        + [dma((n,)) for n in (28, 11, 11, 6, 6, 3, 3, 2, 2, 4, 4, 3, 3, 3, 3, 4, 4)],
         compiler_params=pltpu.CompilerParams(
             collective_id=0, has_side_effects=True, vmem_limit_bytes=48 * 2**20
         ),
         name="conv_both_ways",
-    )(neighbours, features, occupancy, weight3, cotangent)
+    )(neighbours, features, occupancy, jnp.transpose(weight, (1, 0, 2)), cotangent)
 
     wflat = wtotal[: 27 * outs].astype(F32)
     if not with_weight:
         wflat = lax.psum(wflat, "space")
     scaled = wflat * lax.rsqrt(F32(space_count * blocks * 512))
-    weight_grad = jnp.transpose(scaled.reshape(9, 3, outs, cin), (2, 1, 0, 3)).reshape(outs, 27, cin)
+    weight_grad = jnp.transpose(scaled.reshape(27, outs, cin), (1, 0, 2))
     return (act, input_grad, weight_grad)
 
 

time: 45.7 us -> 46.8 us (1.024)
  other arithmetic: 0.06 us -> 0.97 us
  local copies, waits for them, and re-layouts: 4.85 us -> 5.59 us
  Pallas kernels: 39.9 us -> 39.3 us
    unnamed x11 -> x12, local copies, waits for them, and re-layouts: 3.57 us -> 5.59 us
    transpose x2 -> x0, local copies, waits for them, and re-layouts: 1.06 us -> none  [the longest x1 1.01 us: on_device(): jnp.transpose(scaled.reshape(9, 3, outs, cin), (2, 1, 0, 3))]
    mul x1, other arithmetic: 0.06 us -> 0.97 us  [on_device(): scaled = wflat * lax.rsqrt(F32(space_count * blocks * 512))]
    pallas_call x1, Pallas kernels: 39.9 us -> 39.3 us  [on_device(): pl.pallas_call(functools.partial(whole_kernel, space_count, with_weight),...]
where the time goes in v3:
time: 46.8 us; the launch traced here: 46.5 us
  Pallas kernels  39.3 us (84%)
  local copies, waits for them, and re-layouts  5.59 us (12%)
  other arithmetic  0.97 us (2%)
  between operations  0.65 us (1%)
    pallas_call x1, Pallas kernels, on_device(): pl.pallas_call(functools.partial(whole_kernel, space_count, with_weight),...  39.3 us
    unnamed x12, local copies, waits for them, and re-layouts  5.59 us
    mul x1, other arithmetic, on_device(): scaled = wflat * lax.rsqrt(F32(space_count * blocks * 512))  0.97 us

profile of v3, /device:TPU:0, one launch (start us, length us, event | category | flops | bytes accessed | tf_op | source)
XLA Modules:
  0.0 46.5 jit_solution(5578063563531267302)
XLA Ops:
  0.6 0.0 copy-start
  0.6 1.0 %copy-done = bf16[64,27,128]{2,0,1:T(8,128)(2,1)S(1)} copy-done((bf16[64,27,128]{2,0,1:T(8,128)(2,1)S(1)}, bf16[64,27,128]{2,0,1:T(8,128)(2,1)}, u32[]{:S(2)}) %copy-start) | copy-done | bytes 442392
  1.6 0.0 copy-start.1
  1.6 0.9 %copy-done.1 = bf16[4,64,512]{2,1,0:T(8,128)(2,1)S(1)} copy-done((bf16[4,64,512]{2,1,0:T(8,128)(2,1)S(1)}, bf16[4,64,512]{2,1,0:T(8,128)(2,1)}, u32[]{:S(2)}) %copy-start.1) | copy-done | bytes 262168
  2.6 0.0 copy-start.2
  2.6 0.9 %copy-done.2 = bf16[4,32,512]{2,1,0:T(8,128)(2,1)S(1)} copy-done((bf16[4,32,512]{2,1,0:T(8,128)(2,1)S(1)}, bf16[4,32,512]{2,1,0:T(8,128)(2,1)}, u32[]{:S(2)}) %copy-start.2) | copy-done | bytes 131096
  3.5 0.0 copy-start.3
  3.5 0.7 %copy-done.3 = s32[4,512]{1,0:T(4,128)S(1)} copy-done((s32[4,512]{1,0:T(4,128)S(1)}, s32[4,512]{1,0:T(4,128)}, u32[]{:S(2)}) %copy-start.3) | copy-done | bytes 8216
  4.2 0.0 copy-start.4
  4.2 0.7 %copy-done.4 = s32[4,26]{1,0:T(4,128)S(1)} copy-done((s32[4,26]{1,0:T(4,128)S(1)}, s32[4,26]{1,0:T(4,128)}, u32[]{:S(2)}) %copy-start.4) | copy-done | bytes 440
  4.9 39.3 %conv_both_ways.1 = (bf16[4,64,512]{2,1,0:T(8,128)(2,1)S(1)}, bf16[4,32,512]{2,1,0:T(8,128)(2,1)S(1)}, bf16[1792,128]{1,0:T(8,128)(2,1)S(1)}) custom-call(s32[4,26]{1,0:T(4,128)S(1)} %copy-done.4, bf16[4,32,512]{2,1,0:T(8,128)(2,1)S(1)} %copy-done.2, s32[4,512]{1,0:T(4,128)S(1)} %copy-done.3, bf16[27,64,128]{2,1,0:T(8,128)(2,1)S(1)} %bitcast.4, ...), custom_call_target="tpu_custom_call" | custom-call | tf_op jit(solution)/shard_map/conv_both_ways/pallas_call | solution.py:385
  44.2 1.0 %convert_multiply_fusion = f32[1728,128]{1,0:T(8,128)} fusion(bf16[1792,128]{1,0:T(8,128)(2,1)S(1)} %get-tuple-element.8), kind=kLoop, calls=%fused_computation | loop fusion | flops 442368 | bytes 1327104 | tf_op jit(solution)/shard_map/mul | solution.py:427
  45.2 0.7 %copy.10 = bf16[4,64,512]{2,1,0:T(8,128)(2,1)} copy(bf16[4,64,512]{2,1,0:T(8,128)(2,1)S(1)} %get-tuple-element.12) | data formatting | bytes 524288
  45.9 0.7 %copy.11 = bf16[4,32,512]{2,1,0:T(8,128)(2,1)} copy(bf16[4,32,512]{2,1,0:T(8,128)(2,1)S(1)} %get-tuple-element.13) | data formatting | bytes 262144
Async XLA Ops:
  0.6 1.0 %copy-start = (bf16[64,27,128]{2,0,1:T(8,128)(2,1)S(1)}, bf16[64,27,128]{2,0,1:T(8,128)(2,1)}, u32[]{:S(2)}) copy-start(bf16[64,27,128]{2,0,1:T(8,128)(2,1)} %param.7) | copy-start | bytes 1327108
  1.6 0.9 %copy-start.1 = (bf16[4,64,512]{2,1,0:T(8,128)(2,1)S(1)}, bf16[4,64,512]{2,1,0:T(8,128)(2,1)}, u32[]{:S(2)}) copy-start(bf16[4,64,512]{2,1,0:T(8,128)(2,1)} %cotangent_hbm.1) | copy-start | bytes 786436
  2.6 0.9 %copy-start.2 = (bf16[4,32,512]{2,1,0:T(8,128)(2,1)S(1)}, bf16[4,32,512]{2,1,0:T(8,128)(2,1)}, u32[]{:S(2)}) copy-start(bf16[4,32,512]{2,1,0:T(8,128)(2,1)} %features_ref.1) | copy-start | bytes 393220
  3.5 0.7 %copy-start.3 = (s32[4,512]{1,0:T(4,128)S(1)}, s32[4,512]{1,0:T(4,128)}, u32[]{:S(2)}) copy-start(s32[4,512]{1,0:T(4,128)} %occupancy_ref.1) | copy-start | bytes 24580
  4.2 0.7 %copy-start.4 = (s32[4,26]{1,0:T(4,128)S(1)}, s32[4,26]{1,0:T(4,128)}, u32[]{:S(2)}) copy-start(s32[4,26]{1,0:T(4,128)} %neighbours_ref.1) | copy-start | bytes 1252

commit v4 on v3

--- a/solution.py
+++ b/solution.py
@@ -25,14 +25,14 @@
     barrier = pltpu.get_barrier_semaphore()
     for peer in peers:
         pl.semaphore_signal(barrier, inc=1, device_id=peer, device_id_type=MESH)
-    pl.semaphore_wait(barrier, len(peers))
+    return lambda: pl.semaphore_wait(barrier, len(peers))
 
 
 def whole_kernel(
     space_count, with_weight,
-    neighbours_ref, features_ref, occupancy_ref, weight_hbm, cotangent_hbm,
+    neighbours_hbm, features_hbm, occupancy_hbm, weight_hbm, cotangent_hbm,
     act_ref, out_ref, wout_ref,
-    weight_ref, cotangent_ref, full, cubes, sums, patches, grad_patches, shifted, wsum,
+    neighbours_ref, features_ref, occupancy_ref, weight_ref, cotangent_ref, full, cubes, sums, patches, grad_patches, shifted, wsum,
     wsend, ybuf, zsend, zbuf, wown, grads, near_buf, kept, passed, far_buf, rim_out, rim_in,
     fetch, load_send, load_recv, near_send, near_recv, far_send, far_recv, rim_send, rim_recv,
     y_send, y_recv, z_send, z_recv, zg_send, zg_recv, yg_send, yg_recv,
@@ -40,11 +40,18 @@
     blocks, share = features_ref.shape[:2]
     outs = cotangent_ref.shape[1]
     slots = blocks + 2
-    fetches = [pltpu.make_async_copy(cotangent_hbm, cotangent_ref, fetch.at[27])]
+    first = [
+        pltpu.make_async_copy(occupancy_hbm, occupancy_ref, fetch.at[28]),
+        pltpu.make_async_copy(features_hbm, features_ref, fetch.at[29]),
+    ]
+    fetches = [
+        pltpu.make_async_copy(neighbours_hbm, neighbours_ref, fetch.at[30]),
+        pltpu.make_async_copy(cotangent_hbm, cotangent_ref, fetch.at[27]),
+    ]
     for n in range(27):
         rows, columns = pl.ds(n // 9 * outs, outs), pl.ds(n % 9 * 128, 128)
         fetches.append(pltpu.make_async_copy(weight_hbm.at[n], weight_ref.at[rows, columns], fetch.at[n]))
-    for each in fetches:
+    for each in first + fetches:
         each.start()
     s, c, before, after, near, far = places(space_count)
     y = lax.rem(s, 2)
@@ -64,13 +71,15 @@
     peers = [(before, c), (after, c), (s, near), (s, far)]
     if with_weight:
         peers += [(lax.rem(s + 2 * d, space_count), c) for d in range(1, 4)]
-    greet(peers)
+    greeted = greet(peers)
 
     def spread(slots_from, piece, slots_to, peer, index):
         return copy(full.at[slots_from, piece], full.at[slots_to, piece], load_send, load_recv, index, peer)
 
     own = pl.ds(1, blocks)
     low, high = 0, blocks + 1
+    for each in first:
+        each.wait()
     for b in (0, blocks - 1, *range(1, blocks - 1)):
         mask = occupancy_ref[b : b + 1].astype(F32)
         full[1 + b, c] = (features_ref[b].astype(F32) * mask).astype(BF16)
@@ -85,6 +94,7 @@
     own_pass = spread(own, far, own, (s, near), 8)
     high_pass = spread(high, far, high, (s, near), 9)
     low_pass = spread(low, far, low, (s, near), 10)
+    greeted()
     for each in (rim_down, rim_up, own_far, own_near):
         each.start()
     cubes[slots] = jnp.zeros((8, 8, 8, 128), F32)
@@ -372,6 +382,14 @@
         each.wait_send()
 
 
+def finish_kernel(scale, act_ref, grad_ref, wgrad_ref, act_out, grad_out, wgrad_out):
+    act_out[...] = act_ref[...]
+    grad_out[...] = grad_ref[...]
+    outs = wgrad_out.shape[1]
+    for n in range(27):
+        wgrad_out[n] = wgrad_ref[outs * n : outs * (n + 1)].astype(F32) * scale
+
+
 def on_device(space_count, features, occupancy, weight, cotangent, neighbours):
     blocks, share = features.shape[:2]
     outs, _, cin = weight.shape
@@ -379,7 +397,6 @@
     with_weight = space_count == 8 and blocks == 4
     height = -(-27 * outs // 128) * 16
     vmem = pl.BlockSpec(memory_space=pltpu.VMEM)
-    smem = pl.BlockSpec(memory_space=pltpu.SMEM)
     dma = pltpu.SemaphoreType.DMA
     grid = (slots, share, 512)
     act, input_grad, wtotal = pl.pallas_call(
@@ -389,9 +406,12 @@
             jax.ShapeDtypeStruct((blocks, share, 512), BF16),
             jax.ShapeDtypeStruct((8 * height, 128), BF16),
         ],
-        in_specs=[smem] + [vmem] * 2 + [pl.BlockSpec(memory_space=pl.ANY)] * 2,
+        in_specs=[pl.BlockSpec(memory_space=pltpu.HBM)] * 5,
         out_specs=[vmem] * 3,
         scratch_shapes=[
+            pltpu.SMEM(neighbours.shape, jnp.int32),
+            pltpu.VMEM(features.shape, BF16),
+            pltpu.VMEM(occupancy.shape, jnp.int32),
             pltpu.VMEM((3 * outs, 9 * cin), BF16),
             pltpu.VMEM(cotangent.shape, BF16),
             pltpu.VMEM((slots, 4, share, 512), BF16),
@@ -414,19 +434,28 @@
             pltpu.VMEM((2, share, 512), BF16),
             pltpu.VMEM((2, share, 512), BF16),
         ]
-        + [dma((n,)) for n in (28, 11, 11, 6, 6, 3, 3, 2, 2, 4, 4, 3, 3, 3, 3, 4, 4)],
+        + [dma((n,)) for n in (31, 11, 11, 6, 6, 3, 3, 2, 2, 4, 4, 3, 3, 3, 3, 4, 4)],
         compiler_params=pltpu.CompilerParams(
-            collective_id=0, has_side_effects=True, vmem_limit_bytes=48 * 2**20
+            collective_id=0, has_side_effects=True, vmem_limit_bytes=63 * 2**20
         ),
         name="conv_both_ways",
     )(neighbours, features, occupancy, jnp.transpose(weight, (1, 0, 2)), cotangent)
 
-    wflat = wtotal[: 27 * outs].astype(F32)
     if not with_weight:
-        wflat = lax.psum(wflat, "space")
-    scaled = wflat * lax.rsqrt(F32(space_count * blocks * 512))
-    weight_grad = jnp.transpose(scaled.reshape(27, outs, cin), (1, 0, 2))
-    return (act, input_grad, weight_grad)
+        wtotal = lax.psum(wtotal.astype(F32), "space")
+    act, input_grad, weight_grad = pl.pallas_call(
+        functools.partial(finish_kernel, (space_count * blocks * 512) ** -0.5),
+        out_shape=[
+            jax.ShapeDtypeStruct(act.shape, BF16),
+            jax.ShapeDtypeStruct(input_grad.shape, BF16),
+            jax.ShapeDtypeStruct((27, outs, cin), F32),
+        ],
+        in_specs=[vmem] * 3,
+        out_specs=[vmem] * 3,
+        compiler_params=pltpu.CompilerParams(vmem_limit_bytes=63 * 2**20),
+        name="finish",
+    )(act, input_grad, wtotal)
+    return (act, input_grad, jnp.transpose(weight_grad, (1, 0, 2)))
 
 
 def solution(mesh):

time: 46.8 us -> 42.7 us (0.912)
  local copies, waits for them, and re-layouts: 5.59 us -> 0 us
  Pallas kernels: 39.3 us -> 41.9 us
  other arithmetic: 0.97 us -> 0 us
    unnamed x12 -> x0, local copies, waits for them, and re-layouts: 5.59 us -> none
    pallas_call x0 -> x1, Pallas kernels: none -> 2.22 us  [on_device(): pl.pallas_call(functools.partial(finish_kernel, (space_count * blocks * 5...]
    mul x1 -> x0, other arithmetic: 0.97 us -> none  [on_device(): scaled = wflat * lax.rsqrt(F32(space_count * blocks * 512))]
where the time goes in v4:
time: 42.7 us; the launch traced here: 42.5 us
  Pallas kernels  41.9 us (98%)
  between operations  0.64 us (1%)
    pallas_call x1, Pallas kernels, on_device(): pl.pallas_call(functools.partial(whole_kernel, space_count, with_weight),...  39.6 us
    pallas_call x1, Pallas kernels, on_device(): pl.pallas_call(functools.partial(finish_kernel, (space_count * blocks * 5...  2.22 us

profile of v4, /device:TPU:0, one launch (start us, length us, event | category | flops | bytes accessed | tf_op | source)
XLA Modules:
  0.0 42.5 jit_solution(6071980653654975315)
XLA Ops:
  0.6 39.6 %conv_both_ways.1 = (bf16[4,64,512]{2,1,0:T(8,128)(2,1)}, bf16[4,32,512]{2,1,0:T(8,128)(2,1)}, bf16[1792,128]{1,0:T(8,128)(2,1)}) custom-call(s32[4,26]{1,0:T(4,128)} %neighbours_hbm.1, bf16[4,32,512]{2,1,0:T(8,128)(2,1)} %features_hbm.1, s32[4,512]{1,0:T(4,128)} %occupancy_hbm.1, bf16[27,64,128]{2,1,0:T(8,128)(2,1)} %bitcast.2, ...), custom_call_target="tpu_custom_call" | custom-call | tf_op jit(solution)/shard_map/conv_both_ways/pallas_call | solution.py:402
  40.3 2.2 %finish.1 = (bf16[4,64,512]{2,1,0:T(8,128)(2,1)}, bf16[4,32,512]{2,1,0:T(8,128)(2,1)}, f32[27,64,128]{2,1,0:T(8,128)}) custom-call(bf16[4,64,512]{2,1,0:T(8,128)(2,1)} %get-tuple-element.9.act_ref, bf16[4,32,512]{2,1,0:T(8,128)(2,1)} %get-tuple-element.10.grad_ref, bf16[1792,128]{1,0:T(8,128)(2,1)} %get-tuple-element.11.wgrad_ref), custom_call_target="tpu_custom_call" | custom-call | tf_op jit(solution)/shard_map/finish/pallas_call | solution.py:446

commit v5 on v4

--- a/solution.py
+++ b/solution.py
@@ -85,17 +85,17 @@
         full[1 + b, c] = (features_ref[b].astype(F32) * mask).astype(BF16)
     rim_down = spread(1, c, high, (before, c), 0)
     rim_up = spread(blocks, c, low, (after, c), 1)
-    own_far = spread(own, c, own, (s, far), 2)
-    own_near = spread(own, c, own, (s, near), 3)
-    high_far = spread(high, c, high, (s, far), 4)
-    low_far = spread(low, c, low, (s, far), 5)
-    high_near = spread(high, c, high, (s, near), 6)
-    low_near = spread(low, c, low, (s, near), 7)
-    own_pass = spread(own, far, own, (s, near), 8)
-    high_pass = spread(high, far, high, (s, near), 9)
-    low_pass = spread(low, far, low, (s, near), 10)
+    own_near = spread(own, c, own, (s, near), 2)
+    high_far = spread(high, c, high, (s, far), 3)
+    low_far = spread(low, c, low, (s, far), 4)
+    high_near = spread(high, c, high, (s, near), 5)
+    low_near = spread(low, c, low, (s, near), 6)
+    high_pass = spread(high, far, high, (s, near), 7)
+    low_pass = spread(low, far, low, (s, near), 8)
+    own_far = [spread(1 + b, c, 1 + b, (s, far), 9 + b) for b in range(blocks)]
+    own_pass = [spread(1 + b, far, 1 + b, (s, near), 9 + blocks + b) for b in range(blocks)]
     greeted()
-    for each in (rim_down, rim_up, own_far, own_near):
+    for each in (rim_down, rim_up, *own_far, own_near):
         each.start()
     cubes[slots] = jnp.zeros((8, 8, 8, 128), F32)
     sums[...] = jnp.zeros(sums.shape, F32)
@@ -103,8 +103,9 @@
     shifted[...] = jnp.zeros(shifted.shape, BF16)
     k = lax.broadcasted_iota(jnp.int32, (10, 8, 128), 1)
     blank = jnp.zeros((1, 8, 128), F32)
-    own_far.wait_recv()
-    own_pass.start()
+    for b in range(blocks):
+        own_far[b].wait_recv()
+        own_pass[b].start()
     rim_down.wait_recv()
     rim_up.wait_recv()
     for each in (high_far, low_far, high_near, low_near):
@@ -116,9 +117,9 @@
     for each in fetches:
         each.wait()
     own_near.wait_recv()
-    own_pass.wait_recv()
-    for slot in range(1, blocks + 1):
-        turn(slot)
+    for b in range(blocks):
+        own_pass[b].wait_recv()
+        turn(1 + b)
 
     def plane_of(row):
         a = -1 if row == 0 else (1 if row == 9 else 0)
@@ -294,9 +295,8 @@
         for index, peer in enumerate((before, after))
     ]
     sent = [
-        rim_down, rim_up, own_far, own_near, high_far, low_far,
-        high_near, low_near, own_pass, high_pass, low_pass,
-    ] + to_near + to_far + rims
+        rim_down, rim_up, own_near, high_far, low_far, high_near, low_near, high_pass, low_pass,
+    ] + own_far + own_pass + to_near + to_far + rims
 
     def flip(slot):
         grads[slot] = sums[slot].reshape(512, 128).T.astype(BF16).reshape(4, share, 512)
@@ -328,10 +328,6 @@
         each.start()
     lax.fori_loop(1, blocks - 1, inner, 0)
 
-    for slot in range(1, blocks + 1):
-        flip(slot)
-    for each in to_near[4:]:
-        each.start()
     if with_weight:
         total = wown[...]
         for j in range(3):
@@ -352,6 +348,10 @@
     else:
         wout_ref[...] = wsend[...]
 
+    for slot in range(1, blocks + 1):
+        flip(slot)
+    for each in to_near[4:]:
+        each.start()
     for index, slot in enumerate((low, high)):
         to_far[index].wait_recv()
         rim_out[index] = (kept[slot] + far_buf[slot].astype(F32)).astype(BF16)
@@ -382,12 +382,29 @@
         each.wait_send()
 
 
-def finish_kernel(scale, act_ref, grad_ref, wgrad_ref, act_out, grad_out, wgrad_out):
-    act_out[...] = act_ref[...]
-    grad_out[...] = grad_ref[...]
+def finish_kernel(
+    scale, act_ref, grad_ref, wgrad_ref, act_out, grad_out, wgrad_out, taken, given, whole, load, save
+):
     outs = wgrad_out.shape[1]
-    for n in range(27):
-        wgrad_out[n] = wgrad_ref[outs * n : outs * (n + 1)].astype(F32) * scale
+    height = 9 * outs
+    copies = [
+        pltpu.make_async_copy(act_ref, act_out, whole.at[0]),
+        pltpu.make_async_copy(grad_ref, grad_out, whole.at[1]),
+    ]
+    loads = [
+        pltpu.make_async_copy(wgrad_ref.at[pl.ds(height * i, height)], taken.at[i], load.at[i]) for i in range(3)
+    ]
+    saves = [
+        pltpu.make_async_copy(given.at[pl.ds(9 * i, 9)], wgrad_out.at[pl.ds(9 * i, 9)], save.at[i]) for i in range(3)
+    ]
+    for each in loads + copies:
+        each.start()
+    for i in range(3):
+        loads[i].wait()
+        given[9 * i : 9 * i + 9] = taken[i].astype(F32).reshape(9, outs, 128) * scale
+        saves[i].start()
+    for each in copies + saves:
+        each.wait()
 
 
 def on_device(space_count, features, occupancy, weight, cotangent, neighbours):
@@ -397,6 +414,7 @@
     with_weight = space_count == 8 and blocks == 4
     height = -(-27 * outs // 128) * 16
     vmem = pl.BlockSpec(memory_space=pltpu.VMEM)
+    hbm = pl.BlockSpec(memory_space=pltpu.HBM)
     dma = pltpu.SemaphoreType.DMA
     grid = (slots, share, 512)
     act, input_grad, wtotal = pl.pallas_call(
@@ -406,7 +424,7 @@
             jax.ShapeDtypeStruct((blocks, share, 512), BF16),
             jax.ShapeDtypeStruct((8 * height, 128), BF16),
         ],
-        in_specs=[pl.BlockSpec(memory_space=pltpu.HBM)] * 5,
+        in_specs=[hbm] * 5,
         out_specs=[vmem] * 3,
         scratch_shapes=[
             pltpu.SMEM(neighbours.shape, jnp.int32),
@@ -434,7 +452,7 @@
             pltpu.VMEM((2, share, 512), BF16),
             pltpu.VMEM((2, share, 512), BF16),
         ]
-        + [dma((n,)) for n in (31, 11, 11, 6, 6, 3, 3, 2, 2, 4, 4, 3, 3, 3, 3, 4, 4)],
+        + [dma((n,)) for n in (31, 9 + 2 * blocks, 9 + 2 * blocks, 6, 6, 3, 3, 2, 2, 4, 4, 3, 3, 3, 3, 4, 4)],
         compiler_params=pltpu.CompilerParams(
             collective_id=0, has_side_effects=True, vmem_limit_bytes=63 * 2**20
         ),
@@ -450,8 +468,13 @@
             jax.ShapeDtypeStruct(input_grad.shape, BF16),
             jax.ShapeDtypeStruct((27, outs, cin), F32),
         ],
-        in_specs=[vmem] * 3,
-        out_specs=[vmem] * 3,
+        in_specs=[hbm] * 3,
+        out_specs=[hbm] * 3,
+        scratch_shapes=[
+            pltpu.VMEM((3, 9 * outs, cin), F32 if not with_weight else BF16),
+            pltpu.VMEM((27, outs, cin), F32),
+            dma((2,)), dma((3,)), dma((3,)),
+        ],
         compiler_params=pltpu.CompilerParams(vmem_limit_bytes=63 * 2**20),
         name="finish",
     )(act, input_grad, wtotal)

time: 42.7 us -> 53.6 us (1.26)
  Pallas kernels: 41.9 us -> 52.7 us
    pallas_call x1, Pallas kernels: 2.22 us -> 13.1 us  [on_device(): pl.pallas_call(functools.partial(finish_kernel, (space_count * blocks * 5...]
where the time goes in v5:
time: 53.6 us; the launch traced here: 53.4 us
  Pallas kernels  52.7 us (98%)
  between operations  0.64 us (1%)
    pallas_call x1, Pallas kernels, on_device(): pl.pallas_call(functools.partial(whole_kernel, space_count, with_weight),...  39.6 us
    pallas_call x1, Pallas kernels, on_device(): pl.pallas_call(functools.partial(finish_kernel, (space_count * blocks * 5...  13.1 us

profile of v5, /device:TPU:0, one launch (start us, length us, event | category | flops | bytes accessed | tf_op | source)
XLA Modules:
  0.0 53.4 jit_solution(10487316908487957996)
XLA Ops:
  0.6 39.6 %conv_both_ways.1 = (bf16[4,64,512]{2,1,0:T(8,128)(2,1)}, bf16[4,32,512]{2,1,0:T(8,128)(2,1)}, bf16[1792,128]{1,0:T(8,128)(2,1)}) custom-call(s32[4,26]{1,0:T(4,128)} %neighbours_hbm.1, bf16[4,32,512]{2,1,0:T(8,128)(2,1)} %features_hbm.1, s32[4,512]{1,0:T(4,128)} %occupancy_hbm.1, bf16[27,64,128]{2,1,0:T(8,128)(2,1)} %bitcast.2, ...), custom_call_target="tpu_custom_call" | custom-call | tf_op jit(solution)/shard_map/conv_both_ways/pallas_call | solution.py:420
  40.3 13.1 %finish.1 = (bf16[4,64,512]{2,1,0:T(8,128)(2,1)}, bf16[4,32,512]{2,1,0:T(8,128)(2,1)}, f32[27,64,128]{2,1,0:T(8,128)}) custom-call(bf16[4,64,512]{2,1,0:T(8,128)(2,1)} %get-tuple-element.9.act_ref, bf16[4,32,512]{2,1,0:T(8,128)(2,1)} %get-tuple-element.10.grad_ref, bf16[1792,128]{1,0:T(8,128)(2,1)} %get-tuple-element.11.wgrad_ref), custom_call_target="tpu_custom_call" | custom-call | tf_op jit(solution)/shard_map/finish/pallas_call | solution.py:464

commit v6 on v5

--- a/solution.py
+++ b/solution.py
@@ -262,19 +262,21 @@
                 )
                 sums[q, i] = sums[q, i] + delta
 
-        if with_weight:
-            to_beside(j).wait_recv()
-            place = lax.rem(z + 1 + j, 4)
-            joined = wsend[cut(y, place)].astype(F32) + ybuf[place].astype(F32)
-
-            @pl.when(j < 3)
-            def _():
-                zsend[j] = joined.astype(BF16)
-                to_level(j).start()
-
-            @pl.when(j == 3)
-            def _():
-                wown[...] = joined
+        if with_weight and rim is None:
+            for step in range(2):
+                chunk = 2 * (j - 2) + step
+                to_beside(chunk).wait_recv()
+                place = lax.rem(z + 1 + chunk, 4)
+                joined = wsend[cut(y, place)].astype(F32) + ybuf[place].astype(F32)
+
+                @pl.when(chunk < 3)
+                def _():
+                    zsend[chunk] = joined.astype(BF16)
+                    to_level(chunk).start()
+
+                @pl.when(chunk == 3)
+                def _():
+                    wown[...] = joined
 
     kin, other = lax.div(c, 2), lax.div(far, 2)
     parts = (low, high, own)
@@ -328,6 +330,10 @@
         each.start()
     lax.fori_loop(1, blocks - 1, inner, 0)
 
+    for slot in range(1, blocks + 1):
+        flip(slot)
+    for each in to_near[4:]:
+        each.start()
     if with_weight:
         total = wown[...]
         for j in range(3):
@@ -348,10 +354,6 @@
     else:
         wout_ref[...] = wsend[...]
 
-    for slot in range(1, blocks + 1):
-        flip(slot)
-    for each in to_near[4:]:
-        each.start()
     for index, slot in enumerate((low, high)):
         to_far[index].wait_recv()
         rim_out[index] = (kept[slot] + far_buf[slot].astype(F32)).astype(BF16)
@@ -383,27 +385,28 @@
 
 
 def finish_kernel(
-    scale, act_ref, grad_ref, wgrad_ref, act_out, grad_out, wgrad_out, taken, given, whole, load, save
+    scale, act_ref, grad_ref, wgrad_ref, act_out, grad_out, wgrad_out,
+    act_buf, grad_buf, taken, given, load, save,
 ):
     outs = wgrad_out.shape[1]
     height = 9 * outs
-    copies = [
-        pltpu.make_async_copy(act_ref, act_out, whole.at[0]),
-        pltpu.make_async_copy(grad_ref, grad_out, whole.at[1]),
-    ]
     loads = [
         pltpu.make_async_copy(wgrad_ref.at[pl.ds(height * i, height)], taken.at[i], load.at[i]) for i in range(3)
     ]
     saves = [
         pltpu.make_async_copy(given.at[pl.ds(9 * i, 9)], wgrad_out.at[pl.ds(9 * i, 9)], save.at[i]) for i in range(3)
     ]
-    for each in loads + copies:
+    for i, (source, held, target) in enumerate(((act_ref, act_buf, act_out), (grad_ref, grad_buf, grad_out))):
+        loads.append(pltpu.make_async_copy(source, held, load.at[3 + i]))
+        saves.append(pltpu.make_async_copy(held, target, save.at[3 + i]))
+    for each in loads:
         each.start()
-    for i in range(3):
+    for i in range(5):
         loads[i].wait()
-        given[9 * i : 9 * i + 9] = taken[i].astype(F32).reshape(9, outs, 128) * scale
+        if i < 3:
+            given[9 * i : 9 * i + 9] = taken[i].astype(F32).reshape(9, outs, 128) * scale
         saves[i].start()
-    for each in copies + saves:
+    for each in saves:
         each.wait()
 
 
@@ -471,9 +474,11 @@
         in_specs=[hbm] * 3,
         out_specs=[hbm] * 3,
         scratch_shapes=[
+            pltpu.VMEM(act.shape, BF16),
+            pltpu.VMEM(input_grad.shape, BF16),
             pltpu.VMEM((3, 9 * outs, cin), F32 if not with_weight else BF16),
             pltpu.VMEM((27, outs, cin), F32),
-            dma((2,)), dma((3,)), dma((3,)),
+            dma((5,)), dma((5,)),
         ],
         compiler_params=pltpu.CompilerParams(vmem_limit_bytes=63 * 2**20),
         name="finish",

time: 53.6 us -> 42.6 us (0.79)
  Pallas kernels: 52.7 us -> 41.8 us
    pallas_call x1, Pallas kernels: 13.1 us -> 2.05 us  [on_device(): pl.pallas_call(functools.partial(finish_kernel, (space_count * blocks * 5...]
where the time goes in v6:
time: 42.6 us; the launch traced here: 42.4 us
  Pallas kernels  41.8 us (98%)
  between operations  0.64 us (2%)
    pallas_call x1, Pallas kernels, on_device(): pl.pallas_call(functools.partial(whole_kernel, space_count, with_weight),...  39.7 us
    pallas_call x1, Pallas kernels, on_device(): pl.pallas_call(functools.partial(finish_kernel, (space_count * blocks * 5...  2.05 us

profile of v6, /device:TPU:0, one launch (start us, length us, event | category | flops | bytes accessed | tf_op | source)
XLA Modules:
  0.0 42.4 jit_solution(17694810915482196635)
XLA Ops:
  0.6 39.7 %conv_both_ways.1 = (bf16[4,64,512]{2,1,0:T(8,128)(2,1)}, bf16[4,32,512]{2,1,0:T(8,128)(2,1)}, bf16[1792,128]{1,0:T(8,128)(2,1)}) custom-call(s32[4,26]{1,0:T(4,128)} %neighbours_hbm.1, bf16[4,32,512]{2,1,0:T(8,128)(2,1)} %features_hbm.1, s32[4,512]{1,0:T(4,128)} %occupancy_hbm.1, bf16[27,64,128]{2,1,0:T(8,128)(2,1)} %bitcast.2, ...), custom_call_target="tpu_custom_call" | custom-call | tf_op jit(solution)/shard_map/conv_both_ways/pallas_call | solution.py:423
  40.4 2.1 %finish.1 = (bf16[4,64,512]{2,1,0:T(8,128)(2,1)}, bf16[4,32,512]{2,1,0:T(8,128)(2,1)}, f32[27,64,128]{2,1,0:T(8,128)}) custom-call(bf16[4,64,512]{2,1,0:T(8,128)(2,1)} %get-tuple-element.9.act_ref, bf16[4,32,512]{2,1,0:T(8,128)(2,1)} %get-tuple-element.10.grad_ref, bf16[1792,128]{1,0:T(8,128)(2,1)} %get-tuple-element.11.wgrad_ref), custom_call_target="tpu_custom_call" | custom-call | tf_op jit(solution)/shard_map/finish/pallas_call | solution.py:467

commit v7 on v4

--- a/solution.py
+++ b/solution.py
@@ -128,11 +128,9 @@
         for number in range(27):
             yield number, (number // 9 - 1, number // 3 % 3 - 1, number % 3 - 1)
 
-    def forward(t, carry):
-        p = lax.rem(t + 1, blocks)
-
-        @pl.when(t == blocks - 2)
-        def _():
+    def build(t):
+        p = (t + 1) % blocks
+        if t == blocks - 2:
             high_far.wait_recv()
             low_far.wait_recv()
             high_pass.start()
@@ -169,15 +167,19 @@
             for b in range(3):
                 for c in range(3):
                     piece = views[c][b : b + 8].reshape(64, 128).astype(BF16)
-                    patches[64 * row : 64 * row + 64, (3 * b + c) * 128 : (3 * b + c + 1) * 128] = piece
-
+                    patches[t % 2, 64 * row : 64 * row + 64, (3 * b + c) * 128 : (3 * b + c + 1) * 128] = piece
+
+    def forward(t):
+        p = (t + 1) % blocks
         product = lax.dot_general(
-            weight_ref[...], patches[...], (((1,), (1,)), ((), ())), preferred_element_type=F32
+            weight_ref[...], patches[t % 2], (((1,), (1,)), ((), ())), preferred_element_type=F32
         )
+        if t + 1 < blocks:
+            build(t + 1)
         pre_act = (
             product[:outs, 0:512] + product[outs : 2 * outs, 64:576] + product[2 * outs :, 128:640]
         )
-        live = occupancy_ref[pl.ds(p, 1)].astype(F32)
+        live = occupancy_ref[p : p + 1].astype(F32)
         sigma = jax.nn.sigmoid(pre_act)
         act_ref[p] = (pre_act * sigma * live).astype(BF16)
         slope = sigma * (1.0 + pre_act * (1.0 - sigma))
@@ -186,10 +188,11 @@
         shifted[p, :outs, 0:512] = grad_pre
         shifted[p, outs : 2 * outs] = jnp.concatenate([half, grad_pre, half], axis=1)
         shifted[p, 2 * outs :, 128:640] = grad_pre
-        wsum[...] += jnp.dot(shifted[p], patches[...], preferred_element_type=F32)
-        return carry
-
-    lax.fori_loop(0, blocks, forward, 0)
+        wsum[...] += jnp.dot(shifted[p], patches[t % 2], preferred_element_type=F32)
+
+    build(0)
+    for t in range(blocks):
+        forward(t)
 
     for n in range(27):
         part = wsum[n // 9 * outs : (n // 9 + 1) * outs, n % 9 * 128 : (n % 9 + 1) * 128]
@@ -382,12 +385,30 @@
         each.wait_send()
 
 
-def finish_kernel(scale, act_ref, grad_ref, wgrad_ref, act_out, grad_out, wgrad_out):
-    act_out[...] = act_ref[...]
-    grad_out[...] = grad_ref[...]
+def finish_kernel(
+    scale, act_ref, grad_ref, wgrad_ref, act_out, grad_out, wgrad_out,
+    act_buf, grad_buf, taken, given, load, save,
+):
     outs = wgrad_out.shape[1]
-    for n in range(27):
-        wgrad_out[n] = wgrad_ref[outs * n : outs * (n + 1)].astype(F32) * scale
+    height = 9 * outs
+    loads = [
+        pltpu.make_async_copy(wgrad_ref.at[pl.ds(height * i, height)], taken.at[i], load.at[i]) for i in range(3)
+    ]
+    saves = [
+        pltpu.make_async_copy(given.at[pl.ds(9 * i, 9)], wgrad_out.at[pl.ds(9 * i, 9)], save.at[i]) for i in range(3)
+    ]
+    for i, (source, held, target) in enumerate(((act_ref, act_buf, act_out), (grad_ref, grad_buf, grad_out))):
+        loads.append(pltpu.make_async_copy(source, held, load.at[3 + i]))
+        saves.append(pltpu.make_async_copy(held, target, save.at[3 + i]))
+    for each in loads:
+        each.start()
+    for i in range(5):
+        loads[i].wait()
+        if i < 3:
+            given[9 * i : 9 * i + 9] = taken[i].astype(F32).reshape(9, outs, 128) * scale
+        saves[i].start()
+    for each in saves:
+        each.wait()
 
 
 def on_device(space_count, features, occupancy, weight, cotangent, neighbours):
@@ -397,6 +418,7 @@
     with_weight = space_count == 8 and blocks == 4
     height = -(-27 * outs // 128) * 16
     vmem = pl.BlockSpec(memory_space=pltpu.VMEM)
+    hbm = pl.BlockSpec(memory_space=pltpu.HBM)
     dma = pltpu.SemaphoreType.DMA
     grid = (slots, share, 512)
     act, input_grad, wtotal = pl.pallas_call(
@@ -406,7 +428,7 @@
             jax.ShapeDtypeStruct((blocks, share, 512), BF16),
             jax.ShapeDtypeStruct((8 * height, 128), BF16),
         ],
-        in_specs=[pl.BlockSpec(memory_space=pltpu.HBM)] * 5,
+        in_specs=[hbm] * 5,
         out_specs=[vmem] * 3,
         scratch_shapes=[
             pltpu.SMEM(neighbours.shape, jnp.int32),
@@ -417,7 +439,7 @@
             pltpu.VMEM((slots, 4, share, 512), BF16),
             pltpu.VMEM((slots + 1, 8, 8, 8, 128), F32),
             pltpu.VMEM((slots, 8, 8, 8, 128), F32),
-            pltpu.VMEM((640, 9 * cin), BF16),
+            pltpu.VMEM((2, 640, 9 * cin), BF16),
             pltpu.VMEM((640, 9 * cin), F32),
             pltpu.VMEM((blocks, 3 * outs, 640), BF16),
             pltpu.VMEM((3 * outs, 9 * cin), F32),
@@ -450,8 +472,15 @@
             jax.ShapeDtypeStruct(input_grad.shape, BF16),
             jax.ShapeDtypeStruct((27, outs, cin), F32),
         ],
-        in_specs=[vmem] * 3,
-        out_specs=[vmem] * 3,
+        in_specs=[hbm] * 3,
+        out_specs=[hbm] * 3,
+        scratch_shapes=[
+            pltpu.VMEM(act.shape, BF16),
+            pltpu.VMEM(input_grad.shape, BF16),
+            pltpu.VMEM((3, 9 * outs, cin), F32 if not with_weight else BF16),
+            pltpu.VMEM((27, outs, cin), F32),
+            dma((5,)), dma((5,)),
+        ],
         compiler_params=pltpu.CompilerParams(vmem_limit_bytes=63 * 2**20),
         name="finish",
     )(act, input_grad, wtotal)

time: 42.7 us -> 42 us (0.984)
  Pallas kernels: 41.9 us -> 41.2 us
    pallas_call x1, Pallas kernels: 39.6 us -> 39.1 us  [on_device(): pl.pallas_call(functools.partial(whole_kernel, space_count, with_weight),...]
where the time goes in v7:
time: 42 us; the launch traced here: 41.8 us
  Pallas kernels  41.2 us (98%)
  between operations  0.64 us (2%)
    pallas_call x1, Pallas kernels, on_device(): pl.pallas_call(functools.partial(whole_kernel, space_count, with_weight),...  39.1 us
    pallas_call x1, Pallas kernels, on_device(): pl.pallas_call(functools.partial(finish_kernel, (space_count * blocks * 5...  2.05 us

profile of v7, /device:TPU:0, one launch (start us, length us, event | category | flops | bytes accessed | tf_op | source)
XLA Modules:
  0.0 41.8 jit_solution(15350862670386392585)
XLA Ops:
  0.6 39.1 %conv_both_ways.1 = (bf16[4,64,512]{2,1,0:T(8,128)(2,1)}, bf16[4,32,512]{2,1,0:T(8,128)(2,1)}, bf16[1792,128]{1,0:T(8,128)(2,1)}) custom-call(s32[4,26]{1,0:T(4,128)} %neighbours_hbm.1, bf16[4,32,512]{2,1,0:T(8,128)(2,1)} %features_hbm.1, s32[4,512]{1,0:T(4,128)} %occupancy_hbm.1, bf16[27,64,128]{2,1,0:T(8,128)(2,1)} %bitcast.2, ...), custom_call_target="tpu_custom_call" | custom-call | tf_op jit(solution)/shard_map/conv_both_ways/pallas_call | solution.py:424
  39.8 2.1 %finish.1 = (bf16[4,64,512]{2,1,0:T(8,128)(2,1)}, bf16[4,32,512]{2,1,0:T(8,128)(2,1)}, f32[27,64,128]{2,1,0:T(8,128)}) custom-call(bf16[4,64,512]{2,1,0:T(8,128)(2,1)} %get-tuple-element.9.act_ref, bf16[4,32,512]{2,1,0:T(8,128)(2,1)} %get-tuple-element.10.grad_ref, bf16[1792,128]{1,0:T(8,128)(2,1)} %get-tuple-element.11.wgrad_ref), custom_call_target="tpu_custom_call" | custom-call | tf_op jit(solution)/shard_map/finish/pallas_call | solution.py:468
